TPU v7x, 32 devices: a whole 2x2x4 slice. The times are simulated.
32 devices in a mesh: rep: 8 (over z, y), shard: 4 (over x, core).
Axes of the slice: x: 2, y: 2, z: 4, core: 2. Of those that a mesh axis runs over, the one named last changes fastest.
Arguments:
- tokens: bfloat16 [32768, 1024], P(('rep', 'shard')), may hold values from -6 to 6
- lengths: int32 [32, 4], P(('rep', 'shard')), may hold values from 0 to 1024, as said below
- routes: int32 [32768, 8], P(('rep', 'shard')), may hold values from 0 to 15, all different within a row; in each aligned block of 1024 rows (0 to 1023, 1024 to 2047, ...) at most 640 rows name the same one
- w_q: bfloat16 [1024, 1024], P('shard'), may hold values from -0.1875 to 0.1875
- w_kv: bfloat16 [1024, 1024], P('shard'), may hold values from -0.1875 to 0.1875
- w_o: bfloat16 [1024, 1024], P('shard'), may hold values from -0.75 to 0.75
- w_router: bfloat16 [1024, 16], P('shard'), may hold values from -0.09375 to 0.09375
- gain_attn: bfloat16 [1024], P('shard'), may hold values from 0.5 to 1.5
- gain_ffn: bfloat16 [1024], P('shard'), may hold values from 0.5 to 1.5
- w_in: bfloat16 [16, 1024, 1024], P('shard'), may hold values from -0.1875 to 0.1875
- w_out: bfloat16 [16, 512, 1024], P('shard'), may hold values from -1 to 1
- cotangent: bfloat16 [32768, 1024], P(('rep', 'shard')), may hold values from -6 to 6
Outputs:
- out: bfloat16 [32768, 1024], P(('rep', 'shard'))
- d_tokens: bfloat16 [32768, 1024], P(('rep', 'shard'))
- d_w_q: float32 [1024, 1024], P('shard')
- d_w_kv: float32 [1024, 1024], P('shard')
- d_w_o: float32 [1024, 1024], P('shard')
- d_w_router: float32 [1024, 16], P('shard')
- d_gain_attn: float32 [1024], P('shard')
- d_gain_ffn: float32 [1024], P('shard')
- d_w_in: float32 [16, 1024, 1024], P('shard')
- d_w_out: float32 [16, 512, 1024], P('shard')
Inputs may be any that keep to these rules, and one draw needn't show every extreme that they name: `lengths`: entry 0 for an unused sequence entry; a pack's sequences, each padded to a multiple of 128 slots, fit its 1024 slots. In every draw some pack holds one sequence of 1024 rows. `routes`: each row names 8 different experts; among the rows of one pack no expert is named more than 640 times, a bound that some block reaches.
All inputs are finite; a program needn't handle non-finite values.
Results may differ from a plain program's by a relative error of at most 0.02.
Values may be sent and summed in bfloat16 or wider, within the bound.
A program may use at most 448 MiB of HBM per device.

v0:
```python
import jax
import jax.numpy as jnp
from jax import lax
from jax.sharding import PartitionSpec as P

HEADS = 16
KV_HEADS = 8
HD = 64
FF = 512
TOP = 8
EXPERTS = 16
BLK = 128
CAP = 640


epsilon = 1e-05
rope_base = 10000.0
neg_fill = -1e30


def layout(lengths, tok_rows, block_rows):
    seq_lens = lengths[0]
    seq_blocks = (seq_lens + block_rows - 1) // block_rows
    seq_starts = block_rows * (jnp.cumsum(seq_blocks) - seq_blocks)
    slot_ids = jnp.arange(tok_rows, dtype=jnp.int32)[:, None]
    member = (
        (slot_ids >= seq_starts[None, :]) & (slot_ids < seq_starts[None, :] + seq_lens[None, :])
    ).astype(jnp.int32)
    is_valid = jnp.sum(member, axis=1)
    numbers = jnp.arange(seq_lens.shape[0], dtype=jnp.int32)
    seq_ids = jnp.sum(member * numbers[None, :], axis=1) + is_valid - 1
    places = jnp.sum(member * (slot_ids - seq_starts[None, :]), axis=1)
    return (is_valid, seq_ids, places)


def rotate(matrix, places, head_count, head_size, direction):
    half_size = head_size // 2
    frequency = rope_base ** (-2.0 * jnp.arange(half_size, dtype=jnp.float32) / head_size)
    angles = places.astype(jnp.float32)[:, None] * frequency[None, :]
    cosine = jnp.cos(angles)[:, None, :]
    sine_part = direction * jnp.sin(angles)[:, None, :]
    shaped = matrix.reshape(matrix.shape[0], head_count, head_size)
    first_half = shaped[:, :, :half_size]
    second_half = shaped[:, :, half_size:]
    turned = jnp.concatenate(
        [
            first_half * cosine - second_half * sine_part,
            second_half * cosine + first_half * sine_part,
        ],
        axis=2,
    )
    return turned.reshape(matrix.shape[0], head_count * head_size)


def visible(lead_row, block_rows, is_valid, seq_ids):
    tok_rows = seq_ids.shape[0]
    query_ids = lead_row + jnp.arange(block_rows, dtype=jnp.int32)
    key_ids = jnp.arange(tok_rows, dtype=jnp.int32)
    query_seq = lax.dynamic_slice_in_dim(seq_ids, lead_row, block_rows, 0)
    causal = key_ids[None, :] <= query_ids[:, None]
    same_seq = (query_seq[:, None] == seq_ids[None, :]) & (is_valid[None, :] > 0)
    return same_seq & causal | (key_ids[None, :] == query_ids[:, None])


def split_heads(q_rot, k_rot, v_val):
    tok_rows = q_rot.shape[0]
    q_group = HEADS // KV_HEADS
    q_heads = q_rot.reshape(tok_rows, KV_HEADS, q_group, HD).transpose(1, 0, 2, 3)
    k_heads = k_rot.reshape(tok_rows, KV_HEADS, HD).transpose(1, 0, 2)
    v_heads = v_val.reshape(tok_rows, KV_HEADS, HD).transpose(1, 0, 2)
    return (q_heads, k_heads, v_heads)


def attend_forward(q_rot, k_rot, v_val, is_valid, seq_ids):
    tok_rows = q_rot.shape[0]
    block_rows = min(512, tok_rows)
    score_scale = HD ** (-0.5)
    q_heads, k_heads, v_heads = split_heads(q_rot, k_rot, v_val)

    def one_head(operands):
        q_one, k_one, v_one = operands
        outputs = []
        log_parts = []
        for lead_row in range(0, tok_rows, block_rows):
            allowed = visible(lead_row, block_rows, is_valid, seq_ids)
            q_rows = q_one[lead_row : lead_row + block_rows]
            raw_scores = (
                jnp.einsum("qgd,kd->gqk", q_rows, k_one, preferred_element_type=jnp.float32)
                * score_scale
            )
            scores = jnp.where(allowed[None], raw_scores, neg_fill)
            row_max = jnp.max(scores, axis=2, keepdims=True)
            shifted = jnp.exp(scores - row_max)
            totals = jnp.sum(shifted, axis=2, keepdims=True)
            attn_probs = (shifted / totals).astype(jnp.bfloat16)
            outputs.append(
                jnp.einsum("gqk,kd->qgd", attn_probs, v_one, preferred_element_type=jnp.float32)
            )
            log_parts.append(row_max[:, :, 0] + jnp.log(totals[:, :, 0]))
        return (jnp.concatenate(outputs, axis=0), jnp.concatenate(log_parts, axis=1))

    attended, log_sums = lax.map(one_head, (q_heads, k_heads, v_heads))
    merged = attended.transpose(1, 0, 2, 3).reshape(tok_rows, HEADS * HD).astype(jnp.bfloat16)
    return (merged, log_sums)


def attend_backward(q_rot, k_rot, v_val, d_attended, log_sums, is_valid, seq_ids):
    tok_rows = q_rot.shape[0]
    block_rows = min(512, tok_rows)
    score_scale = HD ** (-0.5)
    q_heads, k_heads, v_heads = split_heads(q_rot, k_rot, v_val)
    d_heads = d_attended.reshape(tok_rows, KV_HEADS, HEADS // KV_HEADS, HD).transpose(1, 0, 2, 3)

    def one_head(operands):
        q_one, k_one, v_one, d_one, sums_one = operands
        d_keys = jnp.zeros((tok_rows, HD), jnp.float32)
        d_vals = jnp.zeros((tok_rows, HD), jnp.float32)
        d_query_parts = []
        for lead_row in range(0, tok_rows, block_rows):
            allowed = visible(lead_row, block_rows, is_valid, seq_ids)
            q_rows = q_one[lead_row : lead_row + block_rows]
            d_rows = d_one[lead_row : lead_row + block_rows]
            raw_scores = (
                jnp.einsum("qgd,kd->gqk", q_rows, k_one, preferred_element_type=jnp.float32)
                * score_scale
            )
            scores = jnp.where(allowed[None], raw_scores, neg_fill)
            attn_probs = jnp.exp(scores - sums_one[:, lead_row : lead_row + block_rows, None])
            d_probs = jnp.einsum("qgd,kd->gqk", d_rows, v_one, preferred_element_type=jnp.float32)
            inner_sum = jnp.sum(attn_probs * d_probs, axis=2, keepdims=True)
            d_scores = (attn_probs * (d_probs - inner_sum)).astype(jnp.bfloat16)
            d_query_parts.append(
                jnp.einsum("gqk,kd->qgd", d_scores, k_one, preferred_element_type=jnp.float32)
                * score_scale
            )
            d_keys = (
                d_keys
                + jnp.einsum("gqk,qgd->kd", d_scores, q_rows, preferred_element_type=jnp.float32)
                * score_scale
            )
            d_vals = d_vals + jnp.einsum(
                "gqk,qgd->kd",
                attn_probs.astype(jnp.bfloat16),
                d_rows,
                preferred_element_type=jnp.float32,
            )
        return (jnp.concatenate(d_query_parts, axis=0), d_keys, d_vals)

    d_query, d_keys, d_vals = lax.map(one_head, (q_heads, k_heads, v_heads, d_heads, log_sums))
    d_query = d_query.transpose(1, 0, 2, 3).reshape(tok_rows, HEADS * HD)
    d_keys = d_keys.transpose(1, 0, 2).reshape(tok_rows, KV_HEADS * HD)
    d_vals = d_vals.transpose(1, 0, 2).reshape(tok_rows, KV_HEADS * HD)
    return (d_query, d_keys, d_vals)


def expert_apply(inputs, win_part, wout_part):
    both_lin = jnp.einsum("ecd,edf->ecf", inputs, win_part, preferred_element_type=jnp.float32)
    hidden = (jax.nn.silu(both_lin[:, :, :FF]) * both_lin[:, :, FF:]).astype(jnp.bfloat16)
    return jnp.einsum("ecf,efd->ecd", hidden, wout_part, preferred_element_type=jnp.float32).astype(
        jnp.bfloat16
    )


def expert_grads(inputs, d_rows, win_part, wout_part):
    both_lin = jnp.einsum("ecd,edf->ecf", inputs, win_part, preferred_element_type=jnp.float32)
    gate_lin = both_lin[:, :, :FF]
    up_lin = both_lin[:, :, FF:]
    sigmoid_gate = jax.nn.sigmoid(gate_lin)
    active = gate_lin * sigmoid_gate
    hidden = (active * up_lin).astype(jnp.bfloat16)
    d_hidden = jnp.einsum("ecd,efd->ecf", d_rows, wout_part, preferred_element_type=jnp.float32)
    d_gate_lin = d_hidden * up_lin * sigmoid_gate * (1.0 + gate_lin * (1.0 - sigmoid_gate))
    d_both = jnp.concatenate([d_gate_lin, d_hidden * active], axis=2).astype(jnp.bfloat16)
    d_inputs = jnp.einsum(
        "ecf,edf->ecd", d_both, win_part, preferred_element_type=jnp.float32
    ).astype(jnp.bfloat16)
    return (hidden, d_both, d_inputs)


def norm_back(d_normed, normed, gain_vec, inverse_rms):
    scaled = d_normed * gain_vec
    return inverse_rms * (scaled - normed * jnp.mean(scaled * normed, axis=1, keepdims=True))


def local(
    tokens, lengths, routes, w_q, w_kv, w_o, w_router, gain_attn, gain_ffn, w_in, w_out, cotangent
):
    tok_rows = tokens.shape[0]
    model_width = tokens.shape[1]
    kv_width = KV_HEADS * HD
    cap_rows = CAP
    expert_count = EXPERTS
    sentinel = expert_count * cap_rows
    is_valid, seq_ids, places = layout(lengths, tok_rows, BLK)
    valid_rows = is_valid.astype(jnp.float32)[:, None]
    dense_set = (
        lax.all_gather(w_q, "shard", axis=0, tiled=True),
        lax.all_gather(w_kv, "shard", axis=0, tiled=True),
        lax.all_gather(w_o, "shard", axis=0, tiled=True),
        lax.all_gather(w_router, "shard", axis=0, tiled=True),
        lax.all_gather(gain_attn, "shard", axis=0, tiled=True),
        lax.all_gather(gain_ffn, "shard", axis=0, tiled=True),
    )
    q_full, kv_full, o_full, router_full, gain_one, gain_two = dense_set
    x_float = tokens.astype(jnp.float32)
    scale_one = lax.rsqrt(jnp.mean(x_float * x_float, axis=1, keepdims=True) + epsilon)
    normed_one = x_float * scale_one
    x_one = (normed_one * gain_one.astype(jnp.float32)[None, :]).astype(jnp.bfloat16)
    q_lin = jnp.dot(x_one, q_full, preferred_element_type=jnp.float32)
    kv_lin = jnp.dot(x_one, kv_full, preferred_element_type=jnp.float32)
    q_rot = rotate(q_lin, places, HEADS, HD, 1.0).astype(jnp.bfloat16)
    k_rot = rotate(kv_lin[:, :kv_width], places, KV_HEADS, HD, 1.0).astype(jnp.bfloat16)
    v_val = kv_lin[:, kv_width:].astype(jnp.bfloat16)
    attended, log_sums = attend_forward(q_rot, k_rot, v_val, is_valid, seq_ids)
    branch = jnp.dot(attended, o_full, preferred_element_type=jnp.float32)
    mixed_rows = x_float + valid_rows * branch
    scale_two = lax.rsqrt(jnp.mean(mixed_rows * mixed_rows, axis=1, keepdims=True) + epsilon)
    normed_two = mixed_rows * scale_two
    x_two = (normed_two * gain_two.astype(jnp.float32)[None, :]).astype(jnp.bfloat16)
    logits = jnp.dot(x_two, router_full, preferred_element_type=jnp.float32)
    expert_ids = jnp.arange(expert_count, dtype=jnp.int32)
    chosen = (routes[:, :, None] == expert_ids[None, None, :]).astype(jnp.int32)
    chosen_float = chosen.astype(jnp.float32)
    picked = jnp.sum(chosen_float * logits[:, None, :], axis=2)
    gate_probs = jax.nn.softmax(picked, axis=1)
    hit_table = jnp.sum(chosen, axis=1) * is_valid[:, None]
    slot_ranks = jnp.cumsum(hit_table, axis=0) - 1
    slot_of = jnp.sum(chosen * slot_ranks[:, None, :], axis=2)
    flat_ids = jnp.where(is_valid[:, None] > 0, routes * cap_rows + slot_of, sentinel)
    token_ids = jnp.broadcast_to(jnp.arange(tok_rows, dtype=jnp.int32)[:, None], flat_ids.shape)
    slot_source = (
        jnp.full((sentinel + 1,), tok_rows, jnp.int32)
        .at[flat_ids.reshape(-1)]
        .set(token_ids.reshape(-1))[:sentinel]
    )
    slot_gate = (
        jnp.zeros((sentinel + 1,), jnp.float32)
        .at[flat_ids.reshape(-1)]
        .set(gate_probs.reshape(-1))[:sentinel]
    )
    x_two_pad = jnp.concatenate([x_two, jnp.zeros((1, model_width), jnp.bfloat16)], axis=0)
    slot_inputs = x_two_pad[slot_source].reshape(expert_count, cap_rows, model_width)
    win_part = lax.all_gather(w_in, "shard", axis=0, tiled=True)
    wout_part = lax.all_gather(w_out, "shard", axis=0, tiled=True)
    inputs = slot_inputs
    outputs_all = expert_apply(inputs, win_part, wout_part)
    outputs_pad = jnp.concatenate(
        [outputs_all.reshape(sentinel, model_width), jnp.zeros((1, model_width), jnp.bfloat16)],
        axis=0,
    )
    mixture = jnp.zeros_like(mixed_rows)
    for column in range(TOP):
        mixture = mixture + gate_probs[:, column : column + 1] * outputs_pad[
            flat_ids[:, column]
        ].astype(jnp.float32)
    layer_out = (mixed_rows + mixture).astype(jnp.bfloat16)
    dense_set = (
        lax.all_gather(w_q, "shard", axis=0, tiled=True),
        lax.all_gather(w_kv, "shard", axis=0, tiled=True),
        lax.all_gather(w_o, "shard", axis=0, tiled=True),
        lax.all_gather(w_router, "shard", axis=0, tiled=True),
        lax.all_gather(gain_attn, "shard", axis=0, tiled=True),
        lax.all_gather(gain_ffn, "shard", axis=0, tiled=True),
    )
    q_full, kv_full, o_full, router_full, gain_one, gain_two = dense_set
    d_out = cotangent.astype(jnp.float32)
    d_out_pad = jnp.concatenate([d_out, jnp.zeros((1, model_width), jnp.float32)], axis=0)

    def slot_grads(operands):
        sources, weights_here, outputs_here = operands
        picked_rows = d_out_pad[sources]
        return (
            jnp.sum(outputs_here.astype(jnp.float32) * picked_rows, axis=1),
            (weights_here[:, None] * picked_rows).astype(jnp.bfloat16),
        )

    gate_slots, d_slots = lax.map(
        slot_grads,
        (
            slot_source.reshape(expert_count, cap_rows),
            slot_gate.reshape(expert_count, cap_rows),
            outputs_all,
        ),
    )
    gate_pad = jnp.concatenate([gate_slots.reshape(-1), jnp.zeros((1,), jnp.float32)], axis=0)
    d_gates = gate_pad[flat_ids]
    d_picked = gate_probs * (d_gates - jnp.sum(gate_probs * d_gates, axis=1, keepdims=True))
    d_logits = jnp.sum(chosen_float * d_picked[:, :, None], axis=1).astype(jnp.bfloat16)
    d_router = jnp.einsum("td,te->de", x_two, d_logits, preferred_element_type=jnp.float32)
    d_two = jnp.einsum("te,de->td", d_logits, router_full, preferred_element_type=jnp.float32)
    win_part = lax.all_gather(w_in, "shard", axis=0, tiled=True)
    wout_part = lax.all_gather(w_out, "shard", axis=0, tiled=True)
    inputs = slot_inputs
    hidden, d_both, d_inputs = expert_grads(inputs, d_slots, win_part, wout_part)
    grad_in = lax.psum_scatter(
        jnp.einsum("ecd,ecf->edf", slot_inputs, d_both, preferred_element_type=jnp.float32).astype(
            jnp.bfloat16
        ),
        "shard",
        scatter_dimension=0,
        tiled=True,
    )
    grad_out = lax.psum_scatter(
        jnp.einsum("ecf,ecd->efd", hidden, d_slots, preferred_element_type=jnp.float32).astype(
            jnp.bfloat16
        ),
        "shard",
        scatter_dimension=0,
        tiled=True,
    )
    d_inputs_pad = jnp.concatenate(
        [d_inputs.reshape(sentinel, model_width), jnp.zeros((1, model_width), jnp.bfloat16)], axis=0
    )
    for column in range(TOP):
        d_two = d_two + d_inputs_pad[flat_ids[:, column]].astype(jnp.float32)
    d_gain_two = jnp.sum(d_two * normed_two, axis=0)
    d_mixed = d_out + norm_back(d_two, normed_two, gain_two.astype(jnp.float32)[None, :], scale_two)
    d_branch = (valid_rows * d_mixed).astype(jnp.bfloat16)
    d_w_o = jnp.einsum("tq,td->qd", attended, d_branch, preferred_element_type=jnp.float32)
    d_attended = jnp.einsum(
        "td,qd->tq", d_branch, o_full, preferred_element_type=jnp.float32
    ).astype(jnp.bfloat16)
    d_query, d_keys, d_vals = attend_backward(
        q_rot, k_rot, v_val, d_attended, log_sums, is_valid, seq_ids
    )
    d_q_lin = rotate(d_query, places, HEADS, HD, -1.0).astype(jnp.bfloat16)
    d_kv_lin = jnp.concatenate([rotate(d_keys, places, KV_HEADS, HD, -1.0), d_vals], axis=1).astype(
        jnp.bfloat16
    )
    d_w_q = jnp.einsum("td,tq->dq", x_one, d_q_lin, preferred_element_type=jnp.float32)
    d_w_kv = jnp.einsum("td,tq->dq", x_one, d_kv_lin, preferred_element_type=jnp.float32)
    d_one = jnp.einsum(
        "tq,dq->td", d_q_lin, q_full, preferred_element_type=jnp.float32
    ) + jnp.einsum("tq,dq->td", d_kv_lin, kv_full, preferred_element_type=jnp.float32)
    d_gain_one = jnp.sum(d_one * normed_one, axis=0)
    d_tokens = (
        d_mixed + norm_back(d_one, normed_one, gain_one.astype(jnp.float32)[None, :], scale_one)
    ).astype(jnp.bfloat16)
    group_q, group_kv, group_o, group_router, group_gain_one, group_gain_two = (
        lax.psum_scatter(
            d_w_q.astype(jnp.bfloat16), "shard", scatter_dimension=0, tiled=True
        ).astype(jnp.float32),
        lax.psum_scatter(
            d_w_kv.astype(jnp.bfloat16), "shard", scatter_dimension=0, tiled=True
        ).astype(jnp.float32),
        lax.psum_scatter(
            d_w_o.astype(jnp.bfloat16), "shard", scatter_dimension=0, tiled=True
        ).astype(jnp.float32),
        lax.psum_scatter(
            d_router.astype(jnp.bfloat16), "shard", scatter_dimension=0, tiled=True
        ).astype(jnp.float32),
        lax.psum_scatter(
            d_gain_one.astype(jnp.bfloat16), "shard", scatter_dimension=0, tiled=True
        ).astype(jnp.float32),
        lax.psum_scatter(
            d_gain_two.astype(jnp.bfloat16), "shard", scatter_dimension=0, tiled=True
        ).astype(jnp.float32),
    )
    summed = (
        lax.psum(group_q.astype(jnp.bfloat16), "rep").astype(jnp.float32),
        lax.psum(group_kv.astype(jnp.bfloat16), "rep").astype(jnp.float32),
        lax.psum(group_o.astype(jnp.bfloat16), "rep").astype(jnp.float32),
        lax.psum(group_router.astype(jnp.bfloat16), "rep").astype(jnp.float32),
        lax.psum(group_gain_one.astype(jnp.bfloat16), "rep").astype(jnp.float32),
        lax.psum(group_gain_two.astype(jnp.bfloat16), "rep").astype(jnp.float32),
        lax.psum(grad_in, "rep").astype(jnp.float32),
        lax.psum(grad_out, "rep").astype(jnp.float32),
    )
    return (
        layer_out,
        d_tokens,
        summed[0],
        summed[1],
        summed[2],
        summed[3],
        summed[4],
        summed[5],
        summed[6],
        summed[7],
    )


def solution(mesh):
    placed = (
        P(("rep", "shard"), None),
        P(("rep", "shard"), None),
        P(("rep", "shard"), None),
        P("shard", None),
        P("shard", None),
        P("shard", None),
        P("shard", None),
        P("shard"),
        P("shard"),
        P("shard", None, None),
        P("shard", None, None),
        P(("rep", "shard"), None),
    )
    return jax.shard_map(
        local,
        mesh=mesh,
        in_specs=placed,
        out_specs=(
            P(("rep", "shard"), None),
            P(("rep", "shard"), None),
            P("shard", None),
            P("shard", None),
            P("shard", None),
            P("shard", None),
            P("shard"),
            P("shard"),
            P("shard", None, None),
            P("shard", None, None),
        ),
        check_vma=False,
    )
```

profile of v0, /device:TPU:0, one launch (start us, length us, event | category | flops | bytes accessed | tf_op | source)
XLA Modules:
  0.0 2050.5 jit_solution(1168968144459635874)
XLA Ops:
  30.7 30.5 %scatter_custom_fusion = s32[10241]{0:T(1024)S(1)} fusion(s32[8192]{0:T(1024)S(1)} %bitcast.484, s32[8192]{0:T(1024)S(1)} %reshape.881, s32[]{:T(128)} %constant.153.clone.1), kind=kCustom, calls=%fused_computation.253 | custom fusion | bytes 40968 | tf_op jit(solution)/shard_map/scatter | solution.py:234
  91.1 116.2 %while.41 = (s32[]{:T(128)}, bf16[8,1024,2,64]{1,3,2,0:T(8,128)(2,1)}, f32[8,2,1024]{2,1,0:T(2,128)}, bf16[8,1024,64]{1,2,0:T(8,128)(2,1)S(1)}, s32[1024]{0:T(10...) while((s32[]{:T(128)}, ...), condition=%wide.region_10.11_spmd.clone, body=%wide.region_5.10_spmd.sunk.clone | while | flops 568854016 | bytes 47821960 | solution.py:102
  218.3 30.6 %scatter_custom_fusion.1 = f32[10241]{0:T(1024)S(1)} fusion(s32[8192]{0:T(1024)} %bitcast.485, f32[8192]{0:T(1024)S(1)} %reshape.889, f32[]{:T(128)} %constant.98.clone.1), kind=kCustom, calls=%fused_computation.251 | custom fusion | bytes 41476 | tf_op jit(solution)/shard_map/scatter | solution.py:239
  249.0 44.3 %gather_fusion.1 = bf16[10240,1024]{1,0:T(8,128)(2,1)} fusion(bf16[1025,1024]{1,0:T(8,128)(2,1)S(1)} %concatenate.50, s32[10240]{0:T(1024)S(1)} %get-tuple-element.261), kind=kCustom, calls=%fused_computation.1 | custom fusion | bytes 41984000 | tf_op jit(solution)/shard_map/gather | solution.py:242
  293.4 39.5 %fusion.157 = f32[16,640,1024]{2,1,0:T(8,128)} fusion(bf16[16,640,1024]{2,1,0:T(8,128)(2,1)} %bitcast.464, bf16[16,1024,1024]{2,1,0:T(8,128)(2,1)} %all-gather.14.cloned.1.call-done), kind=kOutput, calls=%fused_computation.300 | convolution fusion | flops 21474836480 | bytes 96468992 | tf_op jit(solution)/shard_map/ecd,edf->ecf/dot_general | solution.py:157
  332.8 19.6 multiply_convert_fusion.2
  352.4 41.2 %all-gather.16.cloned.1.call-done = bf16[16,512,1024]{2,1,0:T(8,128)(2,1)} async-done(((bf16[4,512,1024]{2,1,0:T(8,128)(2,1)}), bf16[16,512,1024]{2,1,0:T(8,128)(2,1)}) %all-gather.16.cloned.1.call-update) | async-done | bytes 16777232 | tf_op jit(solution)/shard_map/all_gather | solution.py:244
  393.7 22.0 %convolution_convert_fusion.1 = bf16[16,640,1024]{2,1,0:T(8,128)(2,1)} fusion(bf16[16,640,512]{2,1,0:T(8,128)(2,1)} %multiply_convert_fusion.2, bf16[16,512,1024]{2,1,0:T(8,128)(2,1)} %all-gather.16.cloned.1.call-done), kind=kOutput, calls=%fused_computation.172 | convolution fusion | flops 10747904000 | bytes 48234496 | tf_op jit(solution)/shard_map/ecf,efd->ecd/dot_general | solution.py:159
  415.7 159.2 %while.42 = (s32[]{:T(128)}, f32[16,640]{1,0:T(8,128)S(1)}, bf16[16,640,1024]{2,1,0:T(8,128)(2,1)}, bf16[16,640,1024]{2,1,0:T(8,128)(2,1)}, s32[16,640]{1,0:T(8,...) while((s32[]{:T(128)}, f32[16,640]{1,0:T(8,128)S(1)}, bf16[16,640,1024]{2,1,0:T(8,128)(2,1)}, ...), condition=%wide.region_23.24_spmd.clone, body=%wide.region_21.23_spmd.sunk.clone | while | flops 3279106 | bytes 13142621 | solution.py:277
  574.9 45.7 %gather_fusion.10 = f32[8192]{0:T(1024)S(1)} fusion(f32[10241]{0:T(1024)S(1)} %pad_maximum_fusion.11, s32[8192]{0:T(1024)S(1)} %copy-done.12), kind=kCustom, calls=%fused_computation.10 | custom fusion | bytes 98304 | tf_op jit(solution)/shard_map/gather | solution.py:286
  621.9 40.0 %multiply_convert_fusion.1 = (bf16[16,640,512]{2,1,0:T(8,128)(2,1)}, bf16[16,640,512]{2,1,0:T(8,128)(2,1)}) fusion(f32[16,640,1024]{2,1,0:T(8,128)} %fusion.157, bf16[16,640,1024]{2,1,0:T(8,128)(2,1)} %get-tuple-element.152, bf16[16,512,1024]{2,1,0:T(8,128)(2,1)} %all-gather.16.cloned.1.call-done), kind=kOutput, calls=%fused_computation.166 | convolution fusion | flops 10805575680 | bytes 100663296 | tf_op jit(solution)/shard_map/ecd,efd->ecf/dot_general | solution.py:171
  661.9 38.5 %fusion.112 = bf16[16,640,1024]{2,1,0:T(8,128)(2,1)} fusion(bf16[16,1024,1024]{2,1,0:T(8,128)(2,1)} %all-gather.14.cloned.1.call-done, bf16[16,640,512]{2,1,0:T(8,128)(2,1)} %get-tuple-element.251, bf16[16,640,512]{2,1,0:T(8,128)(2,1)} %get-tuple-element.250), kind=kOutput, calls=%fused_computation.173 | convolution fusion | flops 21527265280 | bytes 75497472 | tf_op jit(solution)/shard_map/ecf,edf->ecd/dot_general | solution.py:174
  700.5 17.2 concatenate.55
  764.0 16.1 gather_fusion.14
  857.7 221.3 %while.43 = (s32[]{:T(128)}, f32[8,1024,2,64]{1,3,2,0:T(8,128)}, f32[8,1024,64]{1,2,0:T(8,128)}, bf16[8,1024,64]{1,2,0:T(8,128)(2,1)}, bf16[8,1024,64]{1,2,0:T(8...) while((s32[]{:T(128)}, f32[8,1024,2,64]{1,3,2,0:T(8,128)}, ...), condition=%wide.region_30.31_spmd.clone, body=%wide.region_27.30_spmd.sunk.clone | while | flops 1380384256 | bytes 122529504 | solution.py:149
  1102.2 24.4 %convolution_convert_fusion.2 = bf16[16,512,1024]{2,1,0:T(8,128)(2,1)} fusion(bf16[16,640,512]{2,1,0:T(8,128)(2,1)} %multiply_convert_fusion.2, bf16[16,640,1024]{2,1,0:T(8,128)(2,1)} %get-tuple-element.152), kind=kOutput, calls=%fused_computation.174 | convolution fusion | flops 10745806848 | bytes 48234496 | tf_op jit(solution)/shard_map/ecf,ecd->efd/dot_general | solution.py:304
  1126.7 41.5 %convolution_convert_fusion = bf16[16,1024,1024]{2,1,0:T(8,128)(2,1)} fusion(bf16[16,640,1024]{2,1,0:T(8,128)(2,1)} %bitcast.465, bf16[16,640,512]{2,1,0:T(8,128)(2,1)} %get-tuple-element.251, bf16[16,640,512]{2,1,0:T(8,128)(2,1)} %get-tuple-element.250), kind=kOutput, calls=%fused_computation.170 | convolution fusion | flops 21533556736 | bytes 75497472 | tf_op jit(solution)/shard_map/ecd,ecf->edf/dot_general | solution.py:296
  1186.8 129.5 %reduce-scatter.17.cloned.1.call-done = bf16[4,512,1024]{2,1,0:T(8,128)(2,1)} async-done(((bf16[16,512,1024]{2,1,0:T(8,128)(2,1)}), bf16[4,512,1024]{2,1,0:T(8,128)(2,1)}) %reduce-scatter.17.cloned.1.call-update) | async-done | bytes 4194320 | tf_op jit(solution)/shard_map/reduce_scatter | solution.py:303
  1316.3 237.4 %reduce-scatter.15.cloned.1.call-done = bf16[4,1024,1024]{2,1,0:T(8,128)(2,1)} async-done(((bf16[16,1024,1024]{2,1,0:T(8,128)(2,1)}), bf16[4,1024,1024]{2,1,0:T(8,128)(2,1)}) %reduce-scatter.15.cloned.1.call-update) | async-done | bytes 8388624 | tf_op jit(solution)/shard_map/reduce_scatter | solution.py:295
  1555.6 17.3 concatenate.51
  1652.3 16.2 gather_fusion.7
  1684.5 16.5 gather_fusion.9
  1734.8 22.5 %all-reduce.6 = (bf16[256,16]{0,1:T(8,128)(2,1)S(1)}, bf16[256]{0:T(256)(128)(2,1)S(1)}, bf16[256]{0:T(256)(128)(2,1)S(1)}) all-reduce(bf16[256,16]{0,1:T(8,128)(2,1)} %reduce-scatter.13.cloned.1.call-done, bf16[256]{0:T(256)(128)(2,1)S(1)} %dynamic-slice.1, ...), channel_id=1, replica_groups=mesh['rep'=8,'shard'=4] {'rep'}, use_global_device_ids=true, to_apply=%region_39.40 | all-reduce | flops 4608 | bytes 18432 | tf_op jit(solution)/shard_map/psum | solution.py:363
  1759.0 264.9 %all-reduce.11.cloned.1.call-done = (bf16[256,1024]{1,0:T(8,128)(2,1)}, bf16[256,1024]{1,0:T(8,128)(2,1)}, bf16[256,1024]{1,0:T(8,128)(2,1)}, bf16[4,1024,1024]{2,1,0:T(8,128)(2,1)}, bf16[4,512,1024]{2,1,0:T(8,128)(2,1)}) async-done(((bf16[256,1024]{1,0:T(8,128)(2,1)}, bf16[256,1024]{1,0:T(8,128)(2,1)}, bf16[256,1024]{1,0:T(8,128)(2,1)}, bf16[4,1024,1024]{2,1,0:T(8,128)(2,1)}, ...) | async-done | bytes 14155792 | tf_op jit(solution)/shard_map/psum | solution.py:360
  (765 shorter events, 876.1 us)
Async XLA Ops:
  7.2 71.2 %all-gather.8.cloned.1.call-start = ((), (), s32[]{:S(2)}) async-start(), calls=%async_computation.6 | async-start | bytes 2621440 | tf_op jit(solution)/shard_map/all_gather | solution.py:198
  7.9 76.2 %all-gather.10.cloned.1.call-start = ((), (), s32[]{:S(2)}) async-start(), calls=%async_computation.7 | async-start | bytes 2621440 | tf_op jit(solution)/shard_map/all_gather | solution.py:197
  8.7 198.7 %all-gather.12.cloned.1.call-start = ((), (), s32[]{:S(2)}) async-start(), calls=%async_computation.8 | async-start | bytes 2621440 | tf_op jit(solution)/shard_map/all_gather | solution.py:199
  9.4 284.0 %all-gather.14.cloned.1.call-start = ((), (), s32[]{:S(2)}) async-start(), calls=%async_computation.9 | async-start | bytes 41943040 | tf_op jit(solution)/shard_map/all_gather | solution.py:243
  10.0 383.6 %all-gather.16.cloned.1.call-start = ((), (), s32[]{:S(2)}) async-start(), calls=%async_computation.10 | async-start | bytes 20971520 | tf_op jit(solution)/shard_map/all_gather | solution.py:244
  10.6 50.6 %copy-start.77 = (bf16[256,16]{0,1:T(8,128)(2,1)S(1)}, bf16[256,16]{0,1:T(8,128)(2,1)}, u32[]{:S(2)}) copy-start(bf16[256,16]{0,1:T(8,128)(2,1)} %param.24) | copy-start | bytes 24580
  10.6 1160.2 %reduce-scatter.9.cloned.1.call-start = ((), (), s32[]{:S(2)}) async-start(), calls=%async_computation.12 | async-start | bytes 2621440 | tf_op jit(solution)/shard_map/reduce_scatter | solution.py:343
  24.1 60.0 %copy-start.72 = (f32[4,1,256]{2,1,0:T(1,128)}, f32[4,1,256]{2,1,0:T(1,128)S(1)}, u32[]{:S(2)}) copy-start(f32[4,1,256]{2,1,0:T(1,128)S(1)} %convert_element_type.293) | copy-start | bytes 12292
  24.6 59.5 %copy-start.74 = (f32[1024]{0:T(1024)}, f32[1024]{0:T(1024)S(1)}, u32[]{:S(2)}) copy-start(f32[1024]{0:T(1024)S(1)} %add_rsqrt_fusion.1) | copy-start | bytes 12292
  24.6 182.7 %copy-start.78 = (f32[1024]{0:T(1024)}, f32[1024]{0:T(1024)S(1)}, u32[]{:S(2)}) copy-start(f32[1024]{0:T(1024)S(1)} %get-tuple-element.281) | copy-start | bytes 12292
  30.0 183.8 %copy-start.50 = (f32[4,1,256]{2,1,0:T(1,128)}, f32[4,1,256]{2,1,0:T(1,128)S(1)}, u32[]{:S(2)}) copy-start(f32[4,1,256]{2,1,0:T(1,128)S(1)} %convert_element_type.294) | copy-start | bytes 12292
  66.6 147.9 %copy-start.40 = (bf16[1024,16]{0,1:T(8,128)(2,1)}, bf16[1024,16]{0,1:T(8,128)(2,1)S(1)}, u32[]{:S(2)}) copy-start(bf16[1024,16]{0,1:T(8,128)(2,1)S(1)} %all_gather.37) | copy-start | bytes 98308
  217.9 75.5 %copy-start.44 = (f32[1024,8]{0,1:T(8,128)}, f32[1024,8]{0,1:T(8,128)S(1)}, u32[]{:S(2)}) copy-start(f32[1024,8]{0,1:T(8,128)S(1)} %fusion.130) | copy-start | bytes 98308
  352.4 63.2 %copy-start.54 = (f32[16,640]{1,0:T(8,128)S(1)}, f32[16,640]{1,0:T(8,128)}, u32[]{:S(2)}) copy-start(f32[16,640]{1,0:T(8,128)} %custom-call.39) | copy-start | bytes 122884
  415.7 159.2 %copy-start.12 = (s32[8192]{0:T(1024)S(1)}, s32[8192]{0:T(1024)}, u32[]{:S(2)}) copy-start(s32[8192]{0:T(1024)} %broadcast_clamp_fusion) | copy-start | bytes 98308
  574.9 46.3 %copy-start.34 = (s32[1024,8]{0,1:T(8,128)S(1)}, s32[1024,8]{0,1:T(8,128)}, u32[]{:S(2)}) copy-start(s32[1024,8]{0,1:T(8,128)} %param.20) | copy-start | bytes 98308
  857.7 221.4 %copy-start.24 = (f32[1024,32]{0,1:T(8,128)S(1)}, f32[1024,32]{0,1:T(8,128)}, u32[]{:S(2)}) copy-start(f32[1024,32]{0,1:T(8,128)} %copy-done.23) | copy-start | bytes 393220
  857.7 221.4 %copy-start.32 = (f32[1024,32]{0,1:T(8,128)S(1)}, f32[1024,32]{0,1:T(8,128)}, u32[]{:S(2)}) copy-start(f32[1024,32]{0,1:T(8,128)} %get-tuple-element.278) | copy-start | bytes 393220
  1086.5 84.4 %reduce-scatter.11.cloned.1.call-start = ((), (), s32[]{:S(2)}) async-start(), calls=%async_computation.13 | async-start | bytes 2621440 | tf_op jit(solution)/shard_map/reduce_scatter | solution.py:346
  1093.1 93.7 %reduce-scatter.7.cloned.1.call-start = ((), (), s32[]{:S(2)}) async-start(), calls=%async_computation.11 | async-start | bytes 2621440 | tf_op jit(solution)/shard_map/reduce_scatter | solution.py:340
  1102.1 214.2 %reduce-scatter.17.cloned.1.call-start = ((), (), s32[]{:S(2)}) async-start(), calls=%async_computation.16 | async-start | bytes 20971520 | tf_op jit(solution)/shard_map/reduce_scatter | solution.py:303
  1126.7 427.0 %reduce-scatter.15.cloned.1.call-start = ((), (), s32[]{:S(2)}) async-start(), calls=%async_computation.15 | async-start | bytes 41943040 | tf_op jit(solution)/shard_map/reduce_scatter | solution.py:295
  1168.2 566.6 %reduce-scatter.13.cloned.1.call-start = ((), (), s32[]{:S(2)}) async-start(), calls=%async_computation.14 | async-start | bytes 40960 | tf_op jit(solution)/shard_map/reduce_scatter | solution.py:349
  1170.8 853.1 %all-reduce.11.cloned.1.call-start = ((), (), s32[]{:S(2)}) async-start(), calls=%async_computation.17 | async-start | bytes 28311552 | tf_op jit(solution)/shard_map/psum | solution.py:360
  (102 other events, 834.6 us)
Sparse Core Ops, SparseCore 0:
  9.6 25.3 all-gather.7
  36.5 22.6 all-gather.9
  60.7 22.5 all-gather.11
  84.7 201.5 all-gather.13
  287.7 105.9 all-gather.15
  1086.6 31.4 reduce-scatter.8
  1120.8 31.4 reduce-scatter.10
  1155.3 31.4 reduce-scatter.6
  1190.1 126.1 reduce-scatter.16
  1318.7 234.8 reduce-scatter.14
  1556.6 19.3 reduce-scatter.12
  1582.0 441.8 all-reduce.10
where the time goes:
time: 2060 us; the launch traced here: 2050 us
  waiting for transfers between devices  692 us (34%)
  local copies, waits for them, and re-layouts  573 us (28%)
  matrix products  496 us (24%)
  other arithmetic  224 us (11%)
  blocking collectives  46.1 us (2%)
    psum x1, waiting for transfers between devices, local(): lax.psum(group_q.astype(jnp.bfloat16), 'rep').astype(jnp.float32)  265 us
    reduce_scatter x1, waiting for transfers between devices, local(): lax.psum_scatter(jnp.einsum('ecd,ecf->edf', slot_inputs, d_both, preferre...  237 us
    reduce_scatter x1, waiting for transfers between devices, local(): lax.psum_scatter(jnp.einsum('ecf,ecd->efd', hidden, d_slots, preferred_el...  130 us
    gather x8, local copies, waits for them, and re-layouts, local(): outputs_pad[flat_ids[:, column]].astype(jnp.float32)  128 us
    gather x8, local copies, waits for them, and re-layouts, local(): d_two = d_two + d_inputs_pad[flat_ids[:, column]].astype(jnp.float32)  125 us
    gather x16, local copies, waits for them, and re-layouts, slot_grads(): picked_rows = d_out_pad[sources]  97.7 us
    dot_general x32, matrix products, one_head(): jnp.einsum('qgd,kd->gqk', q_rows, k_one, preferred_element_type=jnp.float32)  74.2 us
    dot_general x16, matrix products, one_head(): jnp.einsum('qgd,kd->gqk', d_rows, v_one, preferred_element_type=jnp.float32)  56.2 us
  transfers between devices with their start and end apart: 12, of which 5 were waited for; matrix products, arithmetic and copies ran while one was open for 28% of the time, Pallas kernels for 0%

commit v1 on v0

v1 whole, which is shorter than its diff:
```python
import functools

import jax
import jax.numpy as jnp
from jax import lax
from jax.experimental import pallas as pl
from jax.experimental.pallas import tpu as pltpu
from jax.sharding import PartitionSpec as P

HEADS = 16
KV_HEADS = 8
HD = 64
FF = 512
TOP = 8
EXPERTS = 16
BLK = 128


epsilon = 1e-05
rope_base = 10000.0
neg_fill = -1e30


def layout(lengths, tok_rows, block_rows):
    seq_lens = lengths[0]
    seq_blocks = (seq_lens + block_rows - 1) // block_rows
    seq_starts = block_rows * (jnp.cumsum(seq_blocks) - seq_blocks)
    slot_ids = jnp.arange(tok_rows, dtype=jnp.int32)[:, None]
    member = (
        (slot_ids >= seq_starts[None, :]) & (slot_ids < seq_starts[None, :] + seq_lens[None, :])
    ).astype(jnp.int32)
    is_valid = jnp.sum(member, axis=1)
    numbers = jnp.arange(seq_lens.shape[0], dtype=jnp.int32)
    seq_ids = jnp.sum(member * numbers[None, :], axis=1) + is_valid - 1
    places = jnp.sum(member * (slot_ids - seq_starts[None, :]), axis=1)
    return (is_valid, seq_ids, places)


def rotate(matrix, places, head_count, head_size, direction):
    half_size = head_size // 2
    frequency = rope_base ** (-2.0 * jnp.arange(half_size, dtype=jnp.float32) / head_size)
    angles = places.astype(jnp.float32)[:, None] * frequency[None, :]
    cosine = jnp.cos(angles)[:, None, :]
    sine_part = direction * jnp.sin(angles)[:, None, :]
    shaped = matrix.reshape(matrix.shape[0], head_count, head_size)
    first_half = shaped[:, :, :half_size]
    second_half = shaped[:, :, half_size:]
    turned = jnp.concatenate(
        [
            first_half * cosine - second_half * sine_part,
            second_half * cosine + first_half * sine_part,
        ],
        axis=2,
    )
    return turned.reshape(matrix.shape[0], head_count * head_size)


NN = (((1,), (0,)), ((), ()))
NT = (((1,), (1,)), ((), ()))
TN = (((0,), (0,)), ((), ()))
QB = 256


def mm(a, b, dims):
    return lax.dot_general(a, b, dims, preferred_element_type=jnp.float32)


def block_mask(qseq_ref, kseq_ref, lo, hi):
    rows = lo + lax.broadcasted_iota(jnp.int32, (hi - lo, hi), 0)
    cols = lax.broadcasted_iota(jnp.int32, (hi - lo, hi), 1)
    qs = qseq_ref[lo:hi, :]
    ks = kseq_ref[:, 0:hi]
    return ((qs == ks) & (ks >= 0) & (cols <= rows)) | (cols == rows)


def row_probs(q, k, allowed):
    scores = jnp.where(allowed, mm(q, k, NT) * (HD ** (-0.5)), neg_fill)
    shifted = jnp.exp(scores - jnp.max(scores, axis=1, keepdims=True))
    return shifted * (1.0 / jnp.sum(shifted, axis=1, keepdims=True))


def attend_fwd_kernel(qseq_ref, kseq_ref, q_ref, k_ref, v_ref, o_ref):
    rows = q_ref.shape[0]
    step = min(QB, rows)
    for lo in range(0, rows, step):
        hi = lo + step
        allowed = block_mask(qseq_ref, kseq_ref, lo, hi)
        outs = []
        for head in range(4):
            kv = head // 2
            q = q_ref[lo:hi, head * HD : (head + 1) * HD]
            k = k_ref[0:hi, kv * HD : (kv + 1) * HD]
            v = v_ref[0:hi, kv * HD : (kv + 1) * HD]
            probs = row_probs(q, k, allowed).astype(jnp.bfloat16)
            outs.append(mm(probs, v, NN))
        o_ref[lo:hi, :] = jnp.concatenate(outs, axis=1).astype(jnp.bfloat16)


def attend_bwd_kernel(qseq_ref, kseq_ref, q_ref, k_ref, v_ref, d_ref, dq_ref, dk_ref, dv_ref):
    rows = q_ref.shape[0]
    step = min(QB, rows)
    scale = HD ** (-0.5)
    dk_ref[...] = jnp.zeros_like(dk_ref)
    dv_ref[...] = jnp.zeros_like(dv_ref)
    for lo in range(0, rows, step):
        hi = lo + step
        allowed = block_mask(qseq_ref, kseq_ref, lo, hi)
        dqs = []
        dks = []
        dvs = []
        for kv in range(2):
            k = k_ref[0:hi, kv * HD : (kv + 1) * HD]
            v = v_ref[0:hi, kv * HD : (kv + 1) * HD]
            dk = None
            dv = None
            for head in (2 * kv, 2 * kv + 1):
                q = q_ref[lo:hi, head * HD : (head + 1) * HD]
                d = d_ref[lo:hi, head * HD : (head + 1) * HD]
                probs = row_probs(q, k, allowed)
                d_probs = mm(d, v, NT)
                inner = jnp.sum(probs * d_probs, axis=1, keepdims=True)
                d_scores = (probs * (d_probs - inner)).astype(jnp.bfloat16)
                dqs.append(mm(d_scores, k, NN) * scale)
                dk_one = mm(d_scores, q, TN) * scale
                dv_one = mm(probs.astype(jnp.bfloat16), d, TN)
                dk = dk_one if dk is None else dk + dk_one
                dv = dv_one if dv is None else dv + dv_one
            dks.append(dk)
            dvs.append(dv)
        dq_ref[lo:hi, :] = jnp.concatenate(dqs, axis=1)
        dk_ref[0:hi, :] += jnp.concatenate(dks, axis=1)
        dv_ref[0:hi, :] += jnp.concatenate(dvs, axis=1)


def attend_specs(rows):
    return (
        pl.BlockSpec((rows, 1), lambda h: (0, 0)),
        pl.BlockSpec((1, rows), lambda h: (0, 0)),
        pl.BlockSpec((rows, 4 * HD), lambda h: (0, h)),
        pl.BlockSpec((rows, 2 * HD), lambda h: (0, h)),
        pl.BlockSpec((rows, 2 * HD), lambda h: (0, h)),
    )


def attend_forward(q_rot, k_rot, v_val, key_seq):
    rows = q_rot.shape[0]
    specs = attend_specs(rows)
    return pl.pallas_call(
        attend_fwd_kernel,
        grid=(KV_HEADS // 2,),
        in_specs=list(specs),
        out_specs=specs[2],
        out_shape=jax.ShapeDtypeStruct(q_rot.shape, jnp.bfloat16),
        compiler_params=pltpu.CompilerParams(vmem_limit_bytes=48 * 2**20),
        cost_estimate=pl.CostEstimate(
            flops=16 * HEADS * rows * rows * HD, bytes_accessed=8 * 2**20, transcendentals=0
        ),
    )(key_seq[:, None], key_seq[None, :], q_rot, k_rot, v_val)


def attend_backward(q_rot, k_rot, v_val, d_attended, key_seq):
    rows = q_rot.shape[0]
    specs = attend_specs(rows)
    return pl.pallas_call(
        attend_bwd_kernel,
        grid=(KV_HEADS // 2,),
        in_specs=list(specs) + [specs[2]],
        out_specs=[specs[2], specs[3], specs[4]],
        out_shape=[
            jax.ShapeDtypeStruct(q_rot.shape, jnp.float32),
            jax.ShapeDtypeStruct(k_rot.shape, jnp.float32),
            jax.ShapeDtypeStruct(k_rot.shape, jnp.float32),
        ],
        compiler_params=pltpu.CompilerParams(vmem_limit_bytes=48 * 2**20),
        cost_estimate=pl.CostEstimate(
            flops=40 * HEADS * rows * rows * HD, bytes_accessed=20 * 2**20, transcendentals=0
        ),
    )(key_seq[:, None], key_seq[None, :], q_rot, k_rot, v_val, d_attended)


def expert_kernel(
    lead_ref, x_ref, xt_ref, g_ref, gates_ref, win_ref, wout_ref, mix_in, dx_in,
    mix_ref, dx_ref, dg_ref, dwin_ref, dwout_ref, gh_ref, dgu_ref,
):
    step = pl.program_id(0)

    @pl.when(step == 0)
    def _():
        mix_ref[...] = mix_in[...]
        dx_ref[...] = dx_in[...]
        dg_ref[...] = jnp.zeros_like(dg_ref)

    expert = lead_ref[0] + step
    rows = x_ref.shape[0]
    chunk = min(256, rows)
    for lo in range(0, rows, chunk):
        part = slice(lo, lo + chunk)
        gates = gates_ref[part, :]
        lane = lax.broadcasted_iota(jnp.int32, gates.shape, 1) == expert
        gate = jnp.sum(jnp.where(lane, gates, 0.0), axis=1, keepdims=True)
        both = mm(x_ref[part, :], win_ref[0], NN)
        dh0 = mm(g_ref[part, :], wout_ref[0], NT)
        a = both[:, :FF]
        up = both[:, FF:]
        s = 1.0 / (1.0 + jnp.exp(-a))
        act = a * s
        hid = act * up
        dgate = jnp.sum(hid * dh0, axis=1, keepdims=True)
        dg_ref[part, :] += jnp.where(lane, dgate, 0.0)
        gh = (gate * hid).astype(jnp.bfloat16)
        gh_ref[part, :] = gh
        mix_ref[part, :] += mm(gh, wout_ref[0], NN)
        dh = gate * dh0
        dgu_ref[part, :FF] = (dh * up * (s * (1.0 + a * (1.0 - s)))).astype(jnp.bfloat16)
        dgu_ref[part, FF:] = (dh * act).astype(jnp.bfloat16)
        dx_ref[part, :] += mm(dgu_ref[part, :], win_ref[0], NT)
    width = xt_ref.shape[0]
    for lo in range(0, width, 256):
        part = slice(lo, lo + 256)
        dwin_ref[0, part, :] = mm(xt_ref[part, :], dgu_ref[...], NN).astype(jnp.bfloat16)
    for lo in range(0, FF, 256):
        part = slice(lo, lo + 256)
        dwout_ref[0, part, :] = mm(gh_ref[:, part], g_ref[...], TN).astype(jnp.bfloat16)


def expert_call(lead, x_two, x_turned, cotangent, gates, w_in, w_out, mix, dx):
    rows, width = x_two.shape
    count = w_in.shape[0]
    one = pl.Buffered(1)

    def whole(shape):
        return pl.BlockSpec(shape, lambda e, lead_ref: (0, 0), pipeline_mode=one)

    win_spec = pl.BlockSpec((1,) + w_in.shape[1:], lambda e, lead_ref: (e, 0, 0))
    wout_spec = pl.BlockSpec((1,) + w_out.shape[1:], lambda e, lead_ref: (e, 0, 0))
    full = whole((rows, width))
    return pl.pallas_call(
        expert_kernel,
        grid_spec=pltpu.PrefetchScalarGridSpec(
            num_scalar_prefetch=1,
            grid=(count,),
            in_specs=[
                full, whole((width, rows)), full, whole(gates.shape), win_spec, wout_spec, full, full
            ],
            out_specs=[full, full, whole(gates.shape), win_spec, wout_spec],
            scratch_shapes=[
                pltpu.VMEM((rows, FF), jnp.bfloat16),
                pltpu.VMEM((rows, 2 * FF), jnp.bfloat16),
            ],
        ),
        out_shape=[
            jax.ShapeDtypeStruct(mix.shape, jnp.float32),
            jax.ShapeDtypeStruct(dx.shape, jnp.float32),
            jax.ShapeDtypeStruct(gates.shape, jnp.float32),
            jax.ShapeDtypeStruct(w_in.shape, jnp.bfloat16),
            jax.ShapeDtypeStruct(w_out.shape, jnp.bfloat16),
        ],
        input_output_aliases={7: 0, 8: 1},
        compiler_params=pltpu.CompilerParams(vmem_limit_bytes=58 * 2**20),
        cost_estimate=pl.CostEstimate(
            flops=count * 18 * rows * width * FF,
            bytes_accessed=count * 12 * 2**20 + 24 * 2**20,
            transcendentals=0,
        ),
    )(lead, x_two, x_turned, cotangent, gates, w_in, w_out, mix, dx)


def swap(array, axis, size, bit):
    return lax.ppermute(array, axis, [(i, i ^ bit) for i in range(size)])


def bits_of(size):
    return [1 << b for b in range(size.bit_length() - 1)]


def spread(own, size):
    slots = [own]
    for j in range(1, size):
        low = j & -j
        slots.append(None)
    for bit in reversed(bits_of(size)):
        for j in range(0, size, 2 * bit):
            slots[j + bit] = swap(slots[j], "shard", size, bit)
    return slots


def fold(slots, size):
    slots = list(slots)
    for bit in bits_of(size):
        for j in range(0, size, 2 * bit):
            slots[j] = slots[j] + swap(slots[j + bit], "shard", size, bit)
    return slots[0]


def sum_rep(piece, size):
    me = lax.axis_index("rep")
    for bit in bits_of(size):
        half = piece.shape[0] // 2
        side = (me // bit) % 2
        keep = lax.dynamic_slice_in_dim(piece, side * half, half, 0)
        give = lax.dynamic_slice_in_dim(piece, (1 - side) * half, half, 0)
        piece = keep + swap(give, "rep", size, bit)
    for bit in reversed(bits_of(size)):
        side = (me // bit) % 2
        other = swap(piece, "rep", size, bit)
        first = jnp.where(side == 0, piece, other)
        second = jnp.where(side == 0, other, piece)
        piece = jnp.concatenate([first, second], axis=0)
    return piece


def pack(parts, multiple):
    wide = parts[0].shape[1]
    rows = [parts[0]]
    small = jnp.concatenate([p.reshape(-1) for p in parts[1:]])
    count = -(-small.shape[0] // wide)
    total = -(-(parts[0].shape[0] + count) // multiple) * multiple - parts[0].shape[0]
    small = jnp.pad(small, (0, total * wide - small.shape[0])).reshape(total, wide)
    return jnp.concatenate([parts[0], small], axis=0)


def owned(array, size, slot):
    rows = array.shape[0] // size
    lead = (lax.axis_index("shard") ^ slot) * rows
    return lax.dynamic_slice_in_dim(array, lead, rows, 0).astype(jnp.bfloat16)


def norm_back(d_normed, normed, gain_vec, inverse_rms):
    scaled = d_normed * gain_vec
    return inverse_rms * (scaled - normed * jnp.mean(scaled * normed, axis=1, keepdims=True))


def local(
    n_rep, n_shard,
    tokens, lengths, routes, w_q, w_kv, w_o, w_router, gain_attn, gain_ffn, w_in, w_out, cotangent,
):
    tok_rows = tokens.shape[0]
    kv_width = KV_HEADS * HD
    expert_count = w_in.shape[0] * n_shard
    per_dev = w_in.shape[0]
    is_valid, seq_ids, places = layout(lengths, tok_rows, BLK)
    valid_rows = is_valid.astype(jnp.float32)[:, None]
    key_seq = jnp.where(is_valid > 0, seq_ids, -1)
    q_full, kv_full, o_full, router_full, gain_one, gain_two = (
        lax.all_gather(w_q, "shard", axis=0, tiled=True),
        lax.all_gather(w_kv, "shard", axis=0, tiled=True),
        lax.all_gather(w_o, "shard", axis=0, tiled=True),
        lax.all_gather(w_router, "shard", axis=0, tiled=True),
        lax.all_gather(gain_attn, "shard", axis=0, tiled=True),
        lax.all_gather(gain_ffn, "shard", axis=0, tiled=True),
    )
    gain_one = gain_one.astype(jnp.float32)[None, :]
    gain_two = gain_two.astype(jnp.float32)[None, :]
    win_slots = spread(w_in, n_shard)
    wout_slots = spread(w_out, n_shard)
    x_float = tokens.astype(jnp.float32)
    scale_one = lax.rsqrt(jnp.mean(x_float * x_float, axis=1, keepdims=True) + epsilon)
    normed_one = x_float * scale_one
    x_one = (normed_one * gain_one).astype(jnp.bfloat16)
    q_lin = jnp.dot(x_one, q_full, preferred_element_type=jnp.float32)
    kv_lin = jnp.dot(x_one, kv_full, preferred_element_type=jnp.float32)
    q_rot = rotate(q_lin, places, HEADS, HD, 1.0).astype(jnp.bfloat16)
    k_rot = rotate(kv_lin[:, :kv_width], places, KV_HEADS, HD, 1.0).astype(jnp.bfloat16)
    v_val = kv_lin[:, kv_width:].astype(jnp.bfloat16)
    attended = attend_forward(q_rot, k_rot, v_val, key_seq)
    branch = jnp.dot(attended, o_full, preferred_element_type=jnp.float32)
    mixed_rows = x_float + valid_rows * branch
    scale_two = lax.rsqrt(jnp.mean(mixed_rows * mixed_rows, axis=1, keepdims=True) + epsilon)
    normed_two = mixed_rows * scale_two
    x_two = (normed_two * gain_two).astype(jnp.bfloat16)
    logits = jnp.dot(x_two, router_full, preferred_element_type=jnp.float32)
    expert_ids = jnp.arange(expert_count, dtype=jnp.int32)
    named = jnp.any(routes[:, :, None] == expert_ids[None, None, :], axis=1)
    top_logit = jnp.max(jnp.where(named, logits, -jnp.inf), axis=1, keepdims=True)
    raised = jnp.where(named, jnp.exp(jnp.where(named, logits - top_logit, 0.0)), 0.0)
    gates = valid_rows * (raised / jnp.sum(raised, axis=1, keepdims=True))
    x_turned = x_two.T
    me = lax.axis_index("shard")
    mix = mixed_rows
    dx = jnp.zeros_like(mixed_rows)
    d_gates = jnp.zeros_like(gates)
    gin_slots = [None] * n_shard
    gout_slots = [None] * n_shard
    for j in range(n_shard):
        lead = ((me ^ j) * per_dev).astype(jnp.int32).reshape(1)
        mix, dx, d_part, gin_slots[j], gout_slots[j] = expert_call(
            lead, x_two, x_turned, cotangent, gates, win_slots[j], wout_slots[j], mix, dx
        )
        d_gates = d_gates + d_part
    layer_out = mix.astype(jnp.bfloat16)
    pieces = []
    low = 1
    gin_fold = list(gin_slots)
    gout_fold = list(gout_slots)
    for j in range(0, n_shard, 2):
        moved_in = swap(gin_slots[j + 1], "shard", n_shard, low)
        moved_out = swap(gout_slots[j + 1], "shard", n_shard, low)
        gin_fold[j] = (gin_slots[j], moved_in)
        gout_fold[j] = (gout_slots[j], moved_out)
    for e in range(per_dev):
        slots = [
            jnp.concatenate(
                [
                    gin_fold[j][0][e] + gin_fold[j][1][e],
                    gout_fold[j][0][e] + gout_fold[j][1][e],
                ],
                axis=0,
            )
            for j in range(0, n_shard, 2)
        ]
        for bit in bits_of(n_shard // 2):
            for j in range(0, n_shard // 2, 2 * bit):
                slots[j] = slots[j] + swap(slots[j + bit], "shard", n_shard, 2 * bit)
        pieces.append(sum_rep(slots[0], n_rep))
    width = w_in.shape[1]
    grad_in = jnp.stack([piece[:width] for piece in pieces]).astype(jnp.float32)
    grad_out = jnp.stack([piece[width:] for piece in pieces]).astype(jnp.float32)

    d_out = cotangent.astype(jnp.float32)
    d_logits = (gates * (d_gates - jnp.sum(gates * d_gates, axis=1, keepdims=True))).astype(
        jnp.bfloat16
    )
    d_router = jnp.einsum("td,te->de", x_two, d_logits, preferred_element_type=jnp.float32)
    d_two = dx + jnp.einsum("te,de->td", d_logits, router_full, preferred_element_type=jnp.float32)
    d_gain_two = jnp.sum(d_two * normed_two, axis=0)
    d_mixed = d_out + norm_back(d_two, normed_two, gain_two, scale_two)
    d_branch = (valid_rows * d_mixed).astype(jnp.bfloat16)
    d_w_o = jnp.einsum("tq,td->qd", attended, d_branch, preferred_element_type=jnp.float32)
    d_attended = jnp.einsum(
        "td,qd->tq", d_branch, o_full, preferred_element_type=jnp.float32
    ).astype(jnp.bfloat16)
    early = sum_rep(
        fold(
            [
                pack(
                    [
                        owned(d_w_o, n_shard, j),
                        owned(d_router, n_shard, j),
                        owned(d_gain_two, n_shard, j),
                    ],
                    16 * n_rep,
                )
                for j in range(n_shard)
            ],
            n_shard,
        ),
        n_rep,
    )
    d_query, d_keys, d_vals = attend_backward(q_rot, k_rot, v_val, d_attended, key_seq)
    d_q_lin = rotate(d_query, places, HEADS, HD, -1.0).astype(jnp.bfloat16)
    d_kv_lin = jnp.concatenate([rotate(d_keys, places, KV_HEADS, HD, -1.0), d_vals], axis=1).astype(
        jnp.bfloat16
    )
    d_w_q = jnp.einsum("td,tq->dq", x_one, d_q_lin, preferred_element_type=jnp.float32)
    d_w_kv = jnp.einsum("td,tq->dq", x_one, d_kv_lin, preferred_element_type=jnp.float32)
    d_one = jnp.einsum(
        "tq,dq->td", d_q_lin, q_full, preferred_element_type=jnp.float32
    ) + jnp.einsum("tq,dq->td", d_kv_lin, kv_full, preferred_element_type=jnp.float32)
    d_gain_one = jnp.sum(d_one * normed_one, axis=0)
    d_tokens = (d_mixed + norm_back(d_one, normed_one, gain_one, scale_one)).astype(jnp.bfloat16)
    late = sum_rep(
        fold(
            [
                pack(
                    [
                        jnp.concatenate([owned(d_w_q, n_shard, j), owned(d_w_kv, n_shard, j)], axis=0),
                        owned(d_gain_one, n_shard, j),
                    ],
                    16,
                )
                for j in range(n_shard)
            ],
            n_shard,
        ),
        n_rep,
    )
    own_rows = w_q.shape[0]
    small = early[own_rows:].reshape(-1).astype(jnp.float32)
    router_size = own_rows * expert_count
    return (
        layer_out,
        d_tokens,
        late[:own_rows].astype(jnp.float32),
        late[own_rows : 2 * own_rows].astype(jnp.float32),
        early[:own_rows].astype(jnp.float32),
        small[:router_size].reshape(own_rows, expert_count),
        late[2 * own_rows :].reshape(-1)[:own_rows].astype(jnp.float32),
        small[router_size : router_size + own_rows],
        grad_in,
        grad_out,
    )


def solution(mesh):
    placed = (
        P(("rep", "shard"), None),
        P(("rep", "shard"), None),
        P(("rep", "shard"), None),
        P("shard", None),
        P("shard", None),
        P("shard", None),
        P("shard", None),
        P("shard"),
        P("shard"),
        P("shard", None, None),
        P("shard", None, None),
        P(("rep", "shard"), None),
    )
    return jax.shard_map(
        functools.partial(local, mesh.shape["rep"], mesh.shape["shard"]),
        mesh=mesh,
        in_specs=placed,
        out_specs=(
            P(("rep", "shard"), None),
            P(("rep", "shard"), None),
            P("shard", None),
            P("shard", None),
            P("shard", None),
            P("shard", None),
            P("shard"),
            P("shard"),
            P("shard", None, None),
            P("shard", None, None),
        ),
        check_vma=False,
    )
```

time: 2060 us -> 1480 us (0.72)
  local copies, waits for them, and re-layouts: 573 us -> 59.6 us
  matrix products: 496 us -> 51 us
  Pallas kernels: 0 us -> 299 us
  blocking collectives: 46.1 us -> 312 us
  waiting for transfers between devices: 692 us -> 570 us
  other arithmetic: 224 us -> 125 us
  starting transfers between devices: 0.48 us -> 45.7 us
    ppermute x0 -> x56, waiting for transfers between devices: none -> 568 us  [swap(): return lax.ppermute(array, axis, [(i, i ^ bit) for i in range(size)])]
    gather x36 -> x0, local copies, waits for them, and re-layouts: 441 us -> none  [the longest x8 128 us: local(): outputs_pad[flat_ids[:, column]].astype(jnp.float32)]
    dot_general x118 -> x0, matrix products: 440 us -> none  [the longest x32 74.2 us: one_head(): jnp.einsum('qgd,kd->gqk', q_rows, k_one, preferred_element_type=jnp.float32)]
    reduce_scatter x6 -> x0, waiting for transfers between devices: 383 us -> none  [the longest x1 237 us: local(): lax.psum_scatter(jnp.einsum('ecd,ecf->edf', slot_inputs, d_both, preferre...]
    pallas_call x0 -> x6, Pallas kernels: none -> 299 us  [the longest x4 204 us: expert_call(): pl.pallas_call(expert_kernel, grid_spec=pltpu.PrefetchScalarGridSpec(num_...]
    all_gather x1, blocking collectives: 5.99 us -> 302 us  [local(): lax.all_gather(gain_attn, 'shard', axis=0, tiled=True)]
    psum x1 -> x0, waiting for transfers between devices: 265 us -> none  [local(): lax.psum(group_q.astype(jnp.bfloat16), 'rep').astype(jnp.float32)]
    scatter x2 -> x0, local copies, waits for them, and re-layouts: 61.1 us -> none  [the longest x1 30.6 us: local(): slot_gate = jnp.zeros((sentinel + 1,), jnp.float32).at[flat_ids.reshape(-...]
  transfers between devices with their start and end apart: 12 -> 59, of which waited for: 5 -> 29; matrix products, arithmetic and copies ran while one was open for 28% -> 15% of each run, Pallas kernels for 0% -> 20%
where the time goes in v1:
time: 1480 us
  waiting for transfers between devices  570 us (39%)
  blocking collectives  312 us (21%)
  Pallas kernels  299 us (20%)
  other arithmetic  125 us (8%)
  local copies, waits for them, and re-layouts  59.6 us (4%)
  matrix products  51 us (3%)
  starting transfers between devices  45.7 us (3%)
  between operations  15.6 us (1%)
    ppermute x56, waiting for transfers between devices, swap(): return lax.ppermute(array, axis, [(i, i ^ bit) for i in range(size)])  568 us
    all_gather x1, blocking collectives, local(): lax.all_gather(gain_attn, 'shard', axis=0, tiled=True)  302 us
    pallas_call x4, Pallas kernels, expert_call(): pl.pallas_call(expert_kernel, grid_spec=pltpu.PrefetchScalarGridSpec(num_...  204 us
    pallas_call x1, Pallas kernels, attend_backward(): pl.pallas_call(attend_bwd_kernel, grid=(KV_HEADS // 2,), in_specs=list(sp...  60.5 us
    ppermute x56, starting transfers between devices, swap(): return lax.ppermute(array, axis, [(i, i ^ bit) for i in range(size)])  45.6 us
    pallas_call x1, Pallas kernels, attend_forward(): pl.pallas_call(attend_fwd_kernel, grid=(KV_HEADS // 2,), in_specs=list(sp...  34.1 us
  transfers between devices with their start and end apart: 59, of which 29 were waited for; matrix products, arithmetic and copies ran while one was open for 15% of the time, Pallas kernels for 20%

profile of v1, /device:TPU:0, one launch (start us, length us, event | category | flops | bytes accessed | tf_op | source)
XLA Modules:
  0.0 1477.0 jit_solution(890145295140897017)
XLA Ops:
  15.3 301.6 %all-gather = bf16[4,1,256]{2,1,0:T(2,128)(2,1)S(1)} all-gather(bf16[1,1,256]{2,1,0:T(2,128)(2,1)S(1)} %reshape.330), channel_id=1, replica_groups=mesh['rep'=8,'shard'=4] {'shard'}, dimensions={0}, use_global_device_ids=true | all-gather | bytes 2560 | tf_op jit(solution)/shard_map/all_gather | solution.py:349
  349.5 34.1 %shard_map.195 = bf16[1024,1024]{1,0:T(8,128)(2,1)S(1)} custom-call(s32[1024,1]{1,0:T(8,128)S(1)} %copy.113.qseq_ref, s32[1,1024]{1,0:T(1,128)S(1)} %bitcast.93, bf16[1024,1024]{1,0:T(8,128)(2,1)} %copy.114.q_ref, bf16[1024,512]{1,0:T(8,128)(2,1)S(1)} %copy.115.k_ref, bf16[1024,512]{1,0:T(8,128)(2,1)S(1)} %copy.144.v_ref), custom_call_target="tpu_custom_call" | custom-call | flops 17179869184 | bytes 8388608 | tf_op jit(solution)/shard_map/pallas_call | solution.py:148
  412.5 51.1 %shard_map.196 = (f32[1024,1024]{1,0:T(8,128)}, f32[1024,1024]{1,0:T(8,128)}, f32[1024,16]{1,0:T(8,128)}, bf16[4,1024,1024]{2,1,0:T(8,128)(2,1)}, bf16[4,512,1024]{2,1,0:T(8,128)(2,1)}) custom-call(s32[1]{0:T(128)} %bitcast.14.lead_ref, bf16[1024,1024]{1,0:T(8,128)(2,1)} %copy.123.x_ref, ...), custom_call_target="tpu_custom_call", output_to_operand_aliasing={{0}: (7, {}), {1}: (8, {})} | custom-call | flops 38654705664 | bytes 75497472 | tf_op jit(solution)/shard_map/pallas_call | solution.py:237
  463.6 51.0 %shard_map.197 = (f32[1024,1024]{1,0:T(8,128)}, f32[1024,1024]{1,0:T(8,128)}, f32[1024,16]{1,0:T(8,128)}, bf16[4,1024,1024]{2,1,0:T(8,128)(2,1)}, bf16[4,512,1024]{2,1,0:T(8,128)(2,1)}) custom-call(s32[1]{0:T(128)} %bitcast.13.lead_ref, bf16[1024,1024]{1,0:T(8,128)(2,1)} %copy.123.x_ref, ...), custom_call_target="tpu_custom_call", output_to_operand_aliasing={{0}: (7, {}), {1}: (8, {})} | custom-call | flops 38654705664 | bytes 75497472 | tf_op jit(solution)/shard_map/pallas_call | solution.py:237
  517.8 51.0 %shard_map.198 = (f32[1024,1024]{1,0:T(8,128)}, f32[1024,1024]{1,0:T(8,128)}, f32[1024,16]{1,0:T(8,128)}, bf16[4,1024,1024]{2,1,0:T(8,128)(2,1)}, bf16[4,512,1024]{2,1,0:T(8,128)(2,1)}) custom-call(s32[1]{0:T(128)} %bitcast.12.lead_ref, bf16[1024,1024]{1,0:T(8,128)(2,1)} %copy.123.x_ref, ...), custom_call_target="tpu_custom_call", output_to_operand_aliasing={{0}: (7, {}), {1}: (8, {})} | custom-call | flops 38654705664 | bytes 75497472 | tf_op jit(solution)/shard_map/pallas_call | solution.py:237
  574.2 50.9 %shard_map.199 = (f32[1024,1024]{1,0:T(8,128)}, f32[1024,1024]{1,0:T(8,128)}, f32[1024,16]{1,0:T(8,128)}, bf16[4,1024,1024]{2,1,0:T(8,128)(2,1)}, bf16[4,512,1024]{2,1,0:T(8,128)(2,1)}) custom-call(s32[1]{0:T(128)} %bitcast.lead_ref, bf16[1024,1024]{1,0:T(8,128)(2,1)} %copy.123.x_ref, ...), custom_call_target="tpu_custom_call", output_to_operand_aliasing={{0}: (7, {}), {1}: (8, {})} | custom-call | flops 38654705664 | bytes 75497472 | tf_op jit(solution)/shard_map/pallas_call | solution.py:237
  650.3 60.5 %shard_map.200 = (f32[1024,1024]{1,0:T(8,128)}, f32[1024,512]{1,0:T(8,128)S(1)}, f32[1024,512]{1,0:T(8,128)}) custom-call(s32[1024,1]{1,0:T(8,128)S(1)} %copy.113.qseq_ref, s32[1,1024]{1,0:T(1,128)S(1)} %bitcast.94, bf16[1024,1024]{1,0:T(8,128)(2,1)} %copy.114.q_ref, bf16[1024,512]{1,0:T(8,128)(2,1)S(1)} %copy-done.1, bf16[1024,512]{1,0:T(8,128)(2,1)S(1)} %copy-done.3, ...), custom_call_target="tpu_custom_call" | custom-call | flops 42949672960 | bytes 20971520 | tf_op jit(solution)/shard_map/pallas_call | solution.py:164
  877.7 41.3 %collective-permute-done.28 = bf16[1536,1024]{1,0:T(8,128)(2,1)} collective-permute-done((bf16[1536,1024]{1,0:T(8,128)(2,1)}, bf16[1536,1024]{1,0:T(8,128)(2,1)}, u32[]{:S(2)}, u32[]{:S(2)}) %collective-permute-start.28) | collective-permute-done | bytes 3145760 | tf_op jit(solution)/shard_map/ppermute | solution.py:269
  923.0 63.4 %collective-permute-done.35 = bf16[1536,1024]{1,0:T(8,128)(2,1)} collective-permute-done((bf16[1536,1024]{1,0:T(8,128)(2,1)}, bf16[1536,1024]{1,0:T(8,128)(2,1)}, u32[]{:S(2)}, u32[]{:S(2)}) %collective-permute-start.35) | collective-permute-done | bytes 3145760 | tf_op jit(solution)/shard_map/ppermute | solution.py:269
  990.4 63.4 %collective-permute-done.42 = bf16[1536,1024]{1,0:T(8,128)(2,1)} collective-permute-done((bf16[1536,1024]{1,0:T(8,128)(2,1)}, bf16[1536,1024]{1,0:T(8,128)(2,1)}, u32[]{:S(2)}, u32[]{:S(2)}) %collective-permute-start.42) | collective-permute-done | bytes 3145760 | tf_op jit(solution)/shard_map/ppermute | solution.py:269
  1057.9 60.0 %collective-permute-done.49 = bf16[1536,1024]{1,0:T(8,128)(2,1)} collective-permute-done((bf16[1536,1024]{1,0:T(8,128)(2,1)}, bf16[1536,1024]{1,0:T(8,128)(2,1)}, u32[]{:S(2)}, u32[]{:S(2)}) %collective-permute-start.49) | collective-permute-done | bytes 3145760 | tf_op jit(solution)/shard_map/ppermute | solution.py:269
  1128.4 26.3 %collective-permute-done.50 = bf16[768,1024]{1,0:T(8,128)(2,1)S(1)} collective-permute-done((bf16[768,1024]{1,0:T(8,128)(2,1)S(1)}, bf16[768,1024]{1,0:T(8,128)(2,1)S(1)}, u32[]{:S(2)}, u32[]{:S(2)}) %collective-permute-start.50) | collective-permute-done | bytes 1572896 | tf_op jit(solution)/shard_map/ppermute | solution.py:269
  1158.5 16.0 %collective-permute-done.37 = bf16[384,1024]{1,0:T(8,128)(2,1)S(1)} collective-permute-done((bf16[384,1024]{1,0:T(8,128)(2,1)S(1)}, bf16[384,1024]{1,0:T(8,128)(2,1)S(1)}, u32[]{:S(2)}, u32[]{:S(2)}) %collective-permute-start.37) | collective-permute-done | bytes 786464 | tf_op jit(solution)/shard_map/ppermute | solution.py:269
  1174.9 24.0 %collective-permute-done.44 = bf16[384,1024]{1,0:T(8,128)(2,1)S(1)} collective-permute-done((bf16[384,1024]{1,0:T(8,128)(2,1)S(1)}, bf16[384,1024]{1,0:T(8,128)(2,1)S(1)}, u32[]{:S(2)}, u32[]{:S(2)}) %collective-permute-start.44) | collective-permute-done | bytes 786464 | tf_op jit(solution)/shard_map/ppermute | solution.py:269
  1215.2 40.9 %collective-permute-done.45 = bf16[192,1024]{1,0:T(8,128)(2,1)S(1)} collective-permute-done((bf16[192,1024]{1,0:T(8,128)(2,1)S(1)}, bf16[192,1024]{1,0:T(8,128)(2,1)S(1)}, u32[]{:S(2)}, u32[]{:S(2)}) %collective-permute-start.45) | collective-permute-done | bytes 393248 | tf_op jit(solution)/shard_map/ppermute | solution.py:269
  1256.4 16.6 %collective-permute-done.52 = bf16[192,1024]{1,0:T(8,128)(2,1)S(1)} collective-permute-done((bf16[192,1024]{1,0:T(8,128)(2,1)S(1)}, bf16[192,1024]{1,0:T(8,128)(2,1)S(1)}, u32[]{:S(2)}, u32[]{:S(2)}) %collective-permute-start.52) | collective-permute-done | bytes 393248 | tf_op jit(solution)/shard_map/ppermute | solution.py:269
  1273.2 12.5 collective-permute-done.32
  1307.8 16.7 %collective-permute-done.33 = bf16[384,1024]{1,0:T(8,128)(2,1)S(1)} collective-permute-done((bf16[384,1024]{1,0:T(8,128)(2,1)S(1)}, bf16[384,1024]{1,0:T(8,128)(2,1)S(1)}, u32[]{:S(2)}, u32[]{:S(2)}) %collective-permute-start.33) | collective-permute-done | bytes 786464 | tf_op jit(solution)/shard_map/ppermute | solution.py:269
  1326.5 14.9 %collective-permute-done.40 = bf16[384,1024]{1,0:T(8,128)(2,1)S(1)} collective-permute-done((bf16[384,1024]{1,0:T(8,128)(2,1)S(1)}, bf16[384,1024]{1,0:T(8,128)(2,1)S(1)}, u32[]{:S(2)}, u32[]{:S(2)}) %collective-permute-start.40) | collective-permute-done | bytes 786464 | tf_op jit(solution)/shard_map/ppermute | solution.py:269
  1343.4 14.9 %collective-permute-done.47 = bf16[384,1024]{1,0:T(8,128)(2,1)S(1)} collective-permute-done((bf16[384,1024]{1,0:T(8,128)(2,1)S(1)}, bf16[384,1024]{1,0:T(8,128)(2,1)S(1)}, u32[]{:S(2)}, u32[]{:S(2)}) %collective-permute-start.47) | collective-permute-done | bytes 786464 | tf_op jit(solution)/shard_map/ppermute | solution.py:269
  1360.2 12.7 collective-permute-done.54
  1376.1 20.0 %collective-permute-done.41 = bf16[768,1024]{1,0:T(8,128)(2,1)S(1)} collective-permute-done((bf16[768,1024]{1,0:T(8,128)(2,1)S(1)}, bf16[768,1024]{1,0:T(8,128)(2,1)S(1)}, u32[]{:S(2)}, u32[]{:S(2)}) %collective-permute-start.41) | collective-permute-done | bytes 1572896 | tf_op jit(solution)/shard_map/ppermute | solution.py:269
  1397.2 32.7 %collective-permute-done.48 = bf16[768,1024]{1,0:T(8,128)(2,1)S(1)} collective-permute-done((bf16[768,1024]{1,0:T(8,128)(2,1)S(1)}, bf16[768,1024]{1,0:T(8,128)(2,1)S(1)}, u32[]{:S(2)}, u32[]{:S(2)}) %collective-permute-start.48) | collective-permute-done | bytes 1572896 | tf_op jit(solution)/shard_map/ppermute | solution.py:269
  1430.7 27.5 %collective-permute-done.55 = bf16[768,1024]{1,0:T(8,128)(2,1)S(1)} collective-permute-done((bf16[768,1024]{1,0:T(8,128)(2,1)S(1)}, bf16[768,1024]{1,0:T(8,128)(2,1)S(1)}, u32[]{:S(2)}, u32[]{:S(2)}) %collective-permute-start.55) | collective-permute-done | bytes 1572896 | tf_op jit(solution)/shard_map/ppermute | solution.py:269
  (424 shorter events, 357.5 us)
Async XLA Ops:
  7.2 322.7 %all-gather.8.cloned.1.call-start = ((), (), s32[]{:S(2)}) async-start(), calls=%async_computation.1 | async-start | bytes 2621440 | tf_op jit(solution)/shard_map/all_gather | solution.py:346
  7.9 328.7 %all-gather.6.cloned.1.call-start = ((), (), s32[]{:S(2)}) async-start(), calls=%async_computation | async-start | bytes 2621440 | tf_op jit(solution)/shard_map/all_gather | solution.py:345
  8.7 376.3 %all-gather.10.cloned.1.call-start = ((), (), s32[]{:S(2)}) async-start(), calls=%async_computation.2 | async-start | bytes 2621440 | tf_op jit(solution)/shard_map/all_gather | solution.py:347
  8.7 400.8 %collective-permute-start = (bf16[4,1024,1024]{2,1,0:T(8,128)(2,1)}, bf16[4,1024,1024]{2,1,0:T(8,128)(2,1)}, u32[]{:S(2)}, u32[]{:S(2)}) collective-permute-start(bf16[4,1024,1024]{2,1,0:T(8,128)(2,1)} %win_ref.1), channel_id=1, source_target_pairs={{0,2},{1,3},{2,0},{3,1},{4,6},{5,7},{6,4},{7,5},{8,10},{9,11},{10,... | collective-permute-start | bytes 25165832 | tf_op jit(solution)/shard_map/ppermute | solution.py:269
  11.7 451.9 %collective-permute-start.4 = (bf16[4,1024,1024]{2,1,0:T(8,128)(2,1)}, bf16[4,1024,1024]{2,1,0:T(8,128)(2,1)}, u32[]{:S(2)}, u32[]{:S(2)}) collective-permute-start(bf16[4,1024,1024]{2,1,0:T(8,128)(2,1)} %win_ref.1), channel_id=1, source_target_pairs={{0,1},{1,0},{2,3},{3,2},{4,5},{5,4},{6,7},{7,6},{8,9},{9,8},{10,11... | collective-permute-start | bytes 25165832 | tf_op jit(solution)/shard_map/ppermute | solution.py:269
  11.7 451.8 %collective-permute-start.5 = (bf16[4,512,1024]{2,1,0:T(8,128)(2,1)}, bf16[4,512,1024]{2,1,0:T(8,128)(2,1)}, u32[]{:S(2)}, u32[]{:S(2)}) collective-permute-start(bf16[4,512,1024]{2,1,0:T(8,128)(2,1)} %wout_ref.1), channel_id=1, source_target_pairs={{0,1},{1,0},{2,3},{3,2},{4,5},{5,4},{6,7},{7,6},{8,9},{9,8},{10,11... | collective-permute-start | bytes 12582920 | tf_op jit(solution)/shard_map/ppermute | solution.py:269
  12.2 502.5 %collective-permute-start.2 = (bf16[4,512,1024]{2,1,0:T(8,128)(2,1)}, bf16[4,512,1024]{2,1,0:T(8,128)(2,1)}, u32[]{:S(2)}, u32[]{:S(2)}) collective-permute-start(bf16[4,512,1024]{2,1,0:T(8,128)(2,1)} %wout_ref.1), channel_id=1, source_target_pairs={{0,2},{1,3},{2,0},{3,1},{4,6},{5,7},{6,4},{7,5},{8,10},{9,11},{10,... | collective-permute-start | bytes 12582920 | tf_op jit(solution)/shard_map/ppermute | solution.py:269
  409.5 164.7 %collective-permute-start.1 = (bf16[4,1024,1024]{2,1,0:T(8,128)(2,1)}, bf16[4,1024,1024]{2,1,0:T(8,128)(2,1)}, u32[]{:S(2)}, u32[]{:S(2)}) collective-permute-start(bf16[4,1024,1024]{2,1,0:T(8,128)(2,1)} %collective-permute-done.win_ref), channel_id=1, source_target_pairs={{0,1},{1,0},{2,3},{3,2},{4,5},{5,4},{6,7},{7,6},{8,9},{9,8},{10,11... | collective-permute-start | bytes 25165832 | tf_op jit(solution)/shard_map/ppermute | solution.py:269
  517.7 265.5 %collective-permute-start.24 = (bf16[4,1024,1024]{2,1,0:T(8,128)(2,1)}, bf16[4,1024,1024]{2,1,0:T(8,128)(2,1)}, u32[]{:S(2)}, u32[]{:S(2)}) collective-permute-start(bf16[4,1024,1024]{2,1,0:T(8,128)(2,1)} %get-tuple-element.49), channel_id=1, source_target_pairs={{0,1},{1,0},{2,3},{3,2},{4,5},{5,4},{6,7},{7,6},{8,9},{9,8},{10,11... | collective-permute-start | bytes 25165832 | tf_op jit(solution)/shard_map/ppermute | solution.py:269
  625.1 215.3 %collective-permute-start.26 = (bf16[4,1024,1024]{2,1,0:T(8,128)(2,1)}, bf16[4,1024,1024]{2,1,0:T(8,128)(2,1)}, u32[]{:S(2)}, u32[]{:S(2)}) collective-permute-start(bf16[4,1024,1024]{2,1,0:T(8,128)(2,1)} %get-tuple-element.53), channel_id=1, source_target_pairs={{0,1},{1,0},{2,3},{3,2},{4,5},{5,4},{6,7},{7,6},{8,9},{9,8},{10,11... | collective-permute-start | bytes 25165832 | tf_op jit(solution)/shard_map/ppermute | solution.py:269
  765.4 72.4 %collective-permute-start.27 = (bf16[4,512,1024]{2,1,0:T(8,128)(2,1)}, bf16[4,512,1024]{2,1,0:T(8,128)(2,1)}, u32[]{:S(2)}, u32[]{:S(2)}) collective-permute-start(bf16[4,512,1024]{2,1,0:T(8,128)(2,1)} %get-tuple-element.55), channel_id=1, source_target_pairs={{0,1},{1,0},{2,3},{3,2},{4,5},{5,4},{6,7},{7,6},{8,9},{9,8},{10,11... | collective-permute-start | bytes 12582920 | tf_op jit(solution)/shard_map/ppermute | solution.py:269
  847.6 71.4 %collective-permute-start.28 = (bf16[1536,1024]{1,0:T(8,128)(2,1)}, bf16[1536,1024]{1,0:T(8,128)(2,1)}, u32[]{:S(2)}, u32[]{:S(2)}) collective-permute-start(bf16[1536,1024]{1,0:T(8,128)(2,1)} %pad_maximum_fusion), channel_id=1, source_target_pairs={{0,2},{1,3},{2,0},{3,1},{4,6},{5,7},{6,4},{7,5},{8,10},{9,11},{10,... | collective-permute-start | bytes 9437192 | tf_op jit(solution)/shard_map/ppermute | solution.py:269
  854.7 131.7 %collective-permute-start.35 = (bf16[1536,1024]{1,0:T(8,128)(2,1)}, bf16[1536,1024]{1,0:T(8,128)(2,1)}, u32[]{:S(2)}, u32[]{:S(2)}) collective-permute-start(bf16[1536,1024]{1,0:T(8,128)(2,1)} %pad_maximum_fusion.1), channel_id=1, source_target_pairs={{0,2},{1,3},{2,0},{3,1},{4,6},{5,7},{6,4},{7,5},{8,10},{9,11},{10,... | collective-permute-start | bytes 9437192 | tf_op jit(solution)/shard_map/ppermute | solution.py:269
  860.0 193.8 %collective-permute-start.42 = (bf16[1536,1024]{1,0:T(8,128)(2,1)}, bf16[1536,1024]{1,0:T(8,128)(2,1)}, u32[]{:S(2)}, u32[]{:S(2)}) collective-permute-start(bf16[1536,1024]{1,0:T(8,128)(2,1)} %pad_maximum_fusion.2), channel_id=1, source_target_pairs={{0,2},{1,3},{2,0},{3,1},{4,6},{5,7},{6,4},{7,5},{8,10},{9,11},{10,... | collective-permute-start | bytes 9437192 | tf_op jit(solution)/shard_map/ppermute | solution.py:269
  868.2 249.6 %collective-permute-start.49 = (bf16[1536,1024]{1,0:T(8,128)(2,1)}, bf16[1536,1024]{1,0:T(8,128)(2,1)}, u32[]{:S(2)}, u32[]{:S(2)}) collective-permute-start(bf16[1536,1024]{1,0:T(8,128)(2,1)} %pad_maximum_fusion.3), channel_id=1, source_target_pairs={{0,2},{1,3},{2,0},{3,1},{4,6},{5,7},{6,4},{7,5},{8,10},{9,11},{10,... | collective-permute-start | bytes 9437192 | tf_op jit(solution)/shard_map/ppermute | solution.py:269
  922.6 201.1 %collective-permute-start.29 = (bf16[768,1024]{1,0:T(8,128)(2,1)S(1)}, bf16[768,1024]{1,0:T(8,128)(2,1)S(1)}, u32[]{:S(2)}, u32[]{:S(2)}) collective-permute-start(bf16[768,1024]{1,0:T(8,128)(2,1)S(1)} %constant_dynamic-slice_fusion.11), channel_id=1, source_target_pairs={{0,4},{4,0},{8,12},{12,8},{16,20},{20,16},{24,28},{28,24},{1,5},{5... | collective-permute-start | bytes 4718600 | tf_op jit(solution)/shard_map/ppermute | solution.py:269
  990.0 134.5 %collective-permute-start.36 = (bf16[768,1024]{1,0:T(8,128)(2,1)S(1)}, bf16[768,1024]{1,0:T(8,128)(2,1)S(1)}, u32[]{:S(2)}, u32[]{:S(2)}) collective-permute-start(bf16[768,1024]{1,0:T(8,128)(2,1)S(1)} %constant_dynamic-slice_fusion.8), channel_id=1, source_target_pairs={{0,4},{4,0},{8,12},{12,8},{16,20},{20,16},{24,28},{28,24},{1,5},{5... | collective-permute-start | bytes 4718600 | tf_op jit(solution)/shard_map/ppermute | solution.py:269
  1057.4 70.1 %collective-permute-start.43 = (bf16[768,1024]{1,0:T(8,128)(2,1)S(1)}, bf16[768,1024]{1,0:T(8,128)(2,1)S(1)}, u32[]{:S(2)}, u32[]{:S(2)}) collective-permute-start(bf16[768,1024]{1,0:T(8,128)(2,1)S(1)} %constant_dynamic-slice_fusion.5), channel_id=1, source_target_pairs={{0,4},{4,0},{8,12},{12,8},{16,20},{20,16},{24,28},{28,24},{1,5},{5... | collective-permute-start | bytes 4718600 | tf_op jit(solution)/shard_map/ppermute | solution.py:269
  1128.3 70.6 %collective-permute-start.44 = (bf16[384,1024]{1,0:T(8,128)(2,1)S(1)}, bf16[384,1024]{1,0:T(8,128)(2,1)S(1)}, u32[]{:S(2)}, u32[]{:S(2)}) collective-permute-start(bf16[384,1024]{1,0:T(8,128)(2,1)S(1)} %constant_dynamic-slice_fusion.4), channel_id=1, source_target_pairs={{0,8},{4,12},{8,0},{12,4},{16,24},{20,28},{24,16},{28,20},{1,9},{5... | collective-permute-start | bytes 2359304 | tf_op jit(solution)/shard_map/ppermute | solution.py:269
  1212.0 73.7 %collective-permute-start.32 = (bf16[192,1024]{1,0:T(8,128)(2,1)S(1)}, bf16[192,1024]{1,0:T(8,128)(2,1)S(1)}, u32[]{:S(2)}, u32[]{:S(2)}) collective-permute-start(bf16[192,1024]{1,0:T(8,128)(2,1)S(1)} %dynamic-slice_add_fusion.12), channel_id=1, source_target_pairs={{0,16},{4,20},{8,24},{12,28},{16,0},{20,4},{24,8},{28,12},{1,17},{... | collective-permute-start | bytes 1179656 | tf_op jit(solution)/shard_map/ppermute | solution.py:269
  1215.1 79.0 %collective-permute-start.39 = (bf16[192,1024]{1,0:T(8,128)(2,1)S(1)}, bf16[192,1024]{1,0:T(8,128)(2,1)S(1)}, u32[]{:S(2)}, u32[]{:S(2)}) collective-permute-start(bf16[192,1024]{1,0:T(8,128)(2,1)S(1)} %dynamic-slice_add_fusion.11), channel_id=1, source_target_pairs={{0,16},{4,20},{8,24},{12,28},{16,0},{20,4},{24,8},{28,12},{1,17},{... | collective-permute-start | bytes 1179656 | tf_op jit(solution)/shard_map/ppermute | solution.py:269
  1307.7 65.1 %collective-permute-start.54 = (bf16[384,1024]{1,0:T(8,128)(2,1)S(1)}, bf16[384,1024]{1,0:T(8,128)(2,1)S(1)}, u32[]{:S(2)}, u32[]{:S(2)}) collective-permute-start(bf16[384,1024]{1,0:T(8,128)(2,1)S(1)} %pad_maximum_fusion.26), channel_id=1, source_target_pairs={{0,8},{4,12},{8,0},{12,4},{16,24},{20,28},{24,16},{28,20},{1,9},{5... | collective-permute-start | bytes 2359304 | tf_op jit(solution)/shard_map/ppermute | solution.py:269
  1358.8 71.1 %collective-permute-start.48 = (bf16[768,1024]{1,0:T(8,128)(2,1)S(1)}, bf16[768,1024]{1,0:T(8,128)(2,1)S(1)}, u32[]{:S(2)}, u32[]{:S(2)}) collective-permute-start(bf16[768,1024]{1,0:T(8,128)(2,1)S(1)} %pad_maximum_fusion.13), channel_id=1, source_target_pairs={{0,4},{4,0},{8,12},{12,8},{16,20},{20,16},{24,28},{28,24},{1,5},{5... | collective-permute-start | bytes 4718600 | tf_op jit(solution)/shard_map/ppermute | solution.py:269
  1373.4 84.8 %collective-permute-start.55 = (bf16[768,1024]{1,0:T(8,128)(2,1)S(1)}, bf16[768,1024]{1,0:T(8,128)(2,1)S(1)}, u32[]{:S(2)}, u32[]{:S(2)}) collective-permute-start(bf16[768,1024]{1,0:T(8,128)(2,1)S(1)} %pad_maximum_fusion.14), channel_id=1, source_target_pairs={{0,4},{4,0},{8,12},{12,8},{16,20},{20,16},{24,28},{28,24},{1,5},{5... | collective-permute-start | bytes 4718600 | tf_op jit(solution)/shard_map/ppermute | solution.py:269
  (95 other events, 3651.2 us)
Sparse Core Ops, SparseCore 0:
  9.6 36.6 all-gather.7
  47.8 33.9 all-gather.5
  83.4 33.9 all-gather.9

commit v2 on v1

--- a/solution.py
+++ b/solution.py
@@ -96,7 +96,9 @@
         o_ref[lo:hi, :] = jnp.concatenate(outs, axis=1).astype(jnp.bfloat16)
 
 
-def attend_bwd_kernel(qseq_ref, kseq_ref, q_ref, k_ref, v_ref, d_ref, dq_ref, dk_ref, dv_ref):
+def attend_bwd_kernel(
+    qseq_ref, kseq_ref, q_ref, k_ref, v_ref, d_ref, held_ref, dq_ref, dk_ref, dv_ref
+):
     rows = q_ref.shape[0]
     step = min(QB, rows)
     scale = HD ** (-0.5)
@@ -158,13 +160,13 @@
     )(key_seq[:, None], key_seq[None, :], q_rot, k_rot, v_val)
 
 
-def attend_backward(q_rot, k_rot, v_val, d_attended, key_seq):
+def attend_backward(q_rot, k_rot, v_val, d_attended, key_seq, held):
     rows = q_rot.shape[0]
     specs = attend_specs(rows)
     return pl.pallas_call(
         attend_bwd_kernel,
         grid=(KV_HEADS // 2,),
-        in_specs=list(specs) + [specs[2]],
+        in_specs=list(specs) + [specs[2], pl.BlockSpec(memory_space=pl.ANY)],
         out_specs=[specs[2], specs[3], specs[4]],
         out_shape=[
             jax.ShapeDtypeStruct(q_rot.shape, jnp.float32),
@@ -175,7 +177,7 @@
         cost_estimate=pl.CostEstimate(
             flops=40 * HEADS * rows * rows * HD, bytes_accessed=20 * 2**20, transcendentals=0
         ),
-    )(key_seq[:, None], key_seq[None, :], q_rot, k_rot, v_val, d_attended)
+    )(key_seq[:, None], key_seq[None, :], q_rot, k_rot, v_val, d_attended, held)
 
 
 def expert_kernel(
@@ -284,6 +286,47 @@
     return slots
 
 
+def placed_rows(slots):
+    me = lax.axis_index("shard")
+    rows = slots[0].shape[0]
+    full = jnp.zeros((rows * len(slots), slots[0].shape[1]), slots[0].dtype)
+    for j, slot in enumerate(slots):
+        full = lax.dynamic_update_slice_in_dim(full, slot, (me ^ j) * rows, 0)
+    return full
+
+
+def halve(piece, size, bit):
+    side = (lax.axis_index("rep") // bit) % 2
+    half = piece.shape[0] // 2
+    keep = lax.dynamic_slice_in_dim(piece, side * half, half, 0)
+    give = lax.dynamic_slice_in_dim(piece, (1 - side) * half, half, 0)
+    return keep + swap(give, "rep", size, bit)
+
+
+def rejoin(piece, size, bit):
+    side = (lax.axis_index("rep") // bit) % 2
+    other = swap(piece, "rep", size, bit)
+    first = jnp.where(side == 0, piece, other)
+    second = jnp.where(side == 0, other, piece)
+    return jnp.concatenate([first, second], axis=0)
+
+
+def advance(slots, k, n_rep, n_shard):
+    folds = bits_of(n_shard // 2)
+    rep_bits = bits_of(n_rep)
+    slots = list(slots)
+    if k < len(folds):
+        bit = folds[k]
+        for j in range(0, n_shard // 2, 2 * bit):
+            slots[j] = slots[j] + swap(slots[j + bit], "shard", n_shard, 2 * bit)
+        return slots
+    k -= len(folds)
+    if k < len(rep_bits):
+        return [halve(slots[0], n_rep, rep_bits[k])]
+    k -= len(rep_bits)
+    return [rejoin(slots[0], n_rep, rep_bits[len(rep_bits) - 1 - k])]
+
+
 def fold(slots, size):
     slots = list(slots)
     for bit in bits_of(size):
@@ -341,14 +384,19 @@
     is_valid, seq_ids, places = layout(lengths, tok_rows, BLK)
     valid_rows = is_valid.astype(jnp.float32)[:, None]
     key_seq = jnp.where(is_valid > 0, seq_ids, -1)
-    q_full, kv_full, o_full, router_full, gain_one, gain_two = (
-        lax.all_gather(w_q, "shard", axis=0, tiled=True),
-        lax.all_gather(w_kv, "shard", axis=0, tiled=True),
-        lax.all_gather(w_o, "shard", axis=0, tiled=True),
-        lax.all_gather(w_router, "shard", axis=0, tiled=True),
-        lax.all_gather(gain_attn, "shard", axis=0, tiled=True),
-        lax.all_gather(gain_ffn, "shard", axis=0, tiled=True),
-    )
+    own_rows = w_q.shape[0]
+    dense = spread(
+        pack([jnp.concatenate([w_q, w_kv, w_o], axis=0), w_router, gain_attn, gain_ffn], 16), n_shard
+    )
+    q_full = placed_rows([d[:own_rows] for d in dense])
+    kv_full = placed_rows([d[own_rows : 2 * own_rows] for d in dense])
+    o_full = placed_rows([d[2 * own_rows : 3 * own_rows] for d in dense])
+    rest = [d[3 * own_rows :].reshape(-1) for d in dense]
+    count = own_rows * w_router.shape[1]
+    router_full = placed_rows([r[:count].reshape(w_router.shape) for r in rest])
+    gain_one = placed_rows([r[count : count + own_rows, None] for r in rest])[:, 0]
+    gain_two = placed_rows([r[count + own_rows : count + 2 * own_rows, None] for r in rest])[:, 0]
+    w_in, w_out, q_full = lax.optimization_barrier((w_in, w_out, q_full))
     gain_one = gain_one.astype(jnp.float32)[None, :]
     gain_two = gain_two.astype(jnp.float32)[None, :]
     win_slots = spread(w_in, n_shard)
@@ -408,10 +456,15 @@
             )
             for j in range(0, n_shard, 2)
         ]
-        for bit in bits_of(n_shard // 2):
-            for j in range(0, n_shard // 2, 2 * bit):
-                slots[j] = slots[j] + swap(slots[j + bit], "shard", n_shard, 2 * bit)
-        pieces.append(sum_rep(slots[0], n_rep))
+        pieces.append(slots)
+    held = pieces[0][-1]
+    step_count = len(bits_of(n_shard // 2)) + 2 * len(bits_of(n_rep))
+    for wave in range(step_count + per_dev - 1):
+        for e in range(per_dev):
+            if 0 <= wave - e < step_count:
+                pieces[e] = advance(pieces[e], wave - e, n_rep, n_shard)
+        pieces = lax.optimization_barrier(pieces)
+    pieces = [slots[0] for slots in pieces]
     width = w_in.shape[1]
     grad_in = jnp.stack([piece[:width] for piece in pieces]).astype(jnp.float32)
     grad_out = jnp.stack([piece[width:] for piece in pieces]).astype(jnp.float32)
@@ -446,7 +499,7 @@
         ),
         n_rep,
     )
-    d_query, d_keys, d_vals = attend_backward(q_rot, k_rot, v_val, d_attended, key_seq)
+    d_query, d_keys, d_vals = attend_backward(q_rot, k_rot, v_val, d_attended, key_seq, held)
     d_q_lin = rotate(d_query, places, HEADS, HD, -1.0).astype(jnp.bfloat16)
     d_kv_lin = jnp.concatenate([rotate(d_keys, places, KV_HEADS, HD, -1.0), d_vals], axis=1).astype(
         jnp.bfloat16
@@ -474,7 +527,6 @@
         ),
         n_rep,
     )
-    own_rows = w_q.shape[0]
     small = early[own_rows:].reshape(-1).astype(jnp.float32)
     router_size = own_rows * expert_count
     return (

time: 1480 us -> 1240 us (0.84)
  blocking collectives: 312 us -> 0 us
  local copies, waits for them, and re-layouts: 59.6 us -> 97.8 us
  starting transfers between devices: 45.7 us -> 67.7 us
    all_gather x3 -> x0, blocking collectives: 312 us -> none  [the longest x1 302 us: local(): lax.all_gather(gain_attn, 'shard', axis=0, tiled=True)]
    ppermute x56 -> x59, starting transfers between devices: 45.6 us -> 67.7 us  [swap(): return lax.ppermute(array, axis, [(i, i ^ bit) for i in range(size)])]
    unnamed x131 -> x197, local copies, waits for them, and re-layouts: 18.2 us -> 33 us
    ppermute x56 -> x59, waiting for transfers between devices: 568 us -> 578 us  [swap(): return lax.ppermute(array, axis, [(i, i ^ bit) for i in range(size)])]
  transfers between devices with their start and end apart: 59 -> 59, of which waited for: 29 -> 29; matrix products, arithmetic and copies ran while one was open for 15% -> 19% of each run, Pallas kernels for 20% -> 24%
where the time goes in v2:
time: 1240 us; the launch traced here: 1230 us
  waiting for transfers between devices  578 us (47%)
  Pallas kernels  297 us (24%)
  other arithmetic  135 us (11%)
  local copies, waits for them, and re-layouts  97.8 us (8%)
  starting transfers between devices  67.7 us (5%)
  matrix products  48.9 us (4%)
    ppermute x59, waiting for transfers between devices, swap(): return lax.ppermute(array, axis, [(i, i ^ bit) for i in range(size)])  578 us
    pallas_call x4, Pallas kernels, expert_call(): pl.pallas_call(expert_kernel, grid_spec=pltpu.PrefetchScalarGridSpec(num_...  203 us
    ppermute x59, starting transfers between devices, swap(): return lax.ppermute(array, axis, [(i, i ^ bit) for i in range(size)])  67.7 us
    pallas_call x1, Pallas kernels, attend_backward(): pl.pallas_call(attend_bwd_kernel, grid=(KV_HEADS // 2,), in_specs=list(sp...  60.4 us
    pallas_call x1, Pallas kernels, attend_forward(): pl.pallas_call(attend_fwd_kernel, grid=(KV_HEADS // 2,), in_specs=list(sp...  33.7 us
    unnamed x197, local copies, waits for them, and re-layouts  33 us
  transfers between devices with their start and end apart: 59, of which 29 were waited for; matrix products, arithmetic and copies ran while one was open for 19% of the time, Pallas kernels for 24%

profile of v2, /device:TPU:0, one launch (start us, length us, event | category | flops | bytes accessed | tf_op | source)
XLA Modules:
  0.0 1227.9 jit_solution(6437617519641000236)
XLA Ops:
  15.8 32.2 %collective-permute-done.1 = bf16[784,1024]{1,0:T(8,128)(2,1)} collective-permute-done((bf16[784,1024]{1,0:T(8,128)(2,1)}, bf16[784,1024]{1,0:T(8,128)(2,1)}, u32[]{:S(2)}, u32[]{:S(2)}) %collective-permute-start.1) | collective-permute-done | bytes 1605664 | tf_op jit(solution)/shard_map/ppermute | solution.py:271
  91.5 33.7 %shard_map.195 = bf16[1024,1024]{1,0:T(8,128)(2,1)S(1)} custom-call(s32[1024,1]{1,0:T(8,128)S(1)} %copy.89.qseq_ref, s32[1,1024]{1,0:T(1,128)S(1)} %bitcast.100, bf16[1024,1024]{1,0:T(8,128)(2,1)} %copy.90.q_ref, bf16[1024,512]{1,0:T(8,128)(2,1)S(1)} %copy.91.k_ref, bf16[1024,512]{1,0:T(8,128)(2,1)S(1)} %copy.121.v_ref), custom_call_target="tpu_custom_call" | custom-call | flops 17179869184 | bytes 8388608 | tf_op jit(solution)/shard_map/pallas_call | solution.py:150
  149.5 91.0 %collective-permute-done.3.win_ref = bf16[4,1024,1024]{2,1,0:T(8,128)(2,1)} collective-permute-done((bf16[4,1024,1024]{2,1,0:T(8,128)(2,1)}, bf16[4,1024,1024]{2,1,0:T(8,128)(2,1)}, u32[]{:S(2)}, u32[]{:S(2)}) %collective-permute-start.3) | collective-permute-done | bytes 8388640 | tf_op jit(solution)/shard_map/ppermute | solution.py:271
  243.1 50.8 %shard_map.196 = (f32[1024,1024]{1,0:T(8,128)}, f32[1024,1024]{1,0:T(8,128)}, f32[1024,16]{1,0:T(8,128)}, bf16[4,1024,1024]{2,1,0:T(8,128)(2,1)}, bf16[4,512,1024]{2,1,0:T(8,128)(2,1)}) custom-call(s32[1]{0:T(128)} %bitcast.12.lead_ref, bf16[1024,1024]{1,0:T(8,128)(2,1)} %copy.100.x_ref, ...), custom_call_target="tpu_custom_call", output_to_operand_aliasing={{0}: (7, {}), {1}: (8, {})} | custom-call | flops 38654705664 | bytes 75497472 | tf_op jit(solution)/shard_map/pallas_call | solution.py:239
  293.9 36.1 %collective-permute-done.5.wout_ref = bf16[4,512,1024]{2,1,0:T(8,128)(2,1)} collective-permute-done((bf16[4,512,1024]{2,1,0:T(8,128)(2,1)}, bf16[4,512,1024]{2,1,0:T(8,128)(2,1)}, u32[]{:S(2)}, u32[]{:S(2)}) %collective-permute-start.5) | collective-permute-done | bytes 4194336 | tf_op jit(solution)/shard_map/ppermute | solution.py:271
  330.0 50.7 %shard_map.197 = (f32[1024,1024]{1,0:T(8,128)}, f32[1024,1024]{1,0:T(8,128)}, f32[1024,16]{1,0:T(8,128)}, bf16[4,1024,1024]{2,1,0:T(8,128)(2,1)}, bf16[4,512,1024]{2,1,0:T(8,128)(2,1)}) custom-call(s32[1]{0:T(128)} %bitcast.11.lead_ref, bf16[1024,1024]{1,0:T(8,128)(2,1)} %copy.100.x_ref, ...), custom_call_target="tpu_custom_call", output_to_operand_aliasing={{0}: (7, {}), {1}: (8, {})} | custom-call | flops 38654705664 | bytes 75497472 | tf_op jit(solution)/shard_map/pallas_call | solution.py:239
  381.3 51.0 %shard_map.198 = (f32[1024,1024]{1,0:T(8,128)}, f32[1024,1024]{1,0:T(8,128)}, f32[1024,16]{1,0:T(8,128)}, bf16[4,1024,1024]{2,1,0:T(8,128)(2,1)}, bf16[4,512,1024]{2,1,0:T(8,128)(2,1)}) custom-call(s32[1]{0:T(128)} %bitcast.10.lead_ref, bf16[1024,1024]{1,0:T(8,128)(2,1)} %copy.100.x_ref, ...), custom_call_target="tpu_custom_call", output_to_operand_aliasing={{0}: (7, {}), {1}: (8, {})} | custom-call | flops 38654705664 | bytes 75497472 | tf_op jit(solution)/shard_map/pallas_call | solution.py:239
  432.3 50.8 %shard_map.199 = (f32[1024,1024]{1,0:T(8,128)}, f32[1024,1024]{1,0:T(8,128)}, f32[1024,16]{1,0:T(8,128)}, bf16[4,1024,1024]{2,1,0:T(8,128)(2,1)}, bf16[4,512,1024]{2,1,0:T(8,128)(2,1)}) custom-call(s32[1]{0:T(128)} %bitcast.lead_ref, bf16[1024,1024]{1,0:T(8,128)(2,1)} %copy.100.x_ref, ...), custom_call_target="tpu_custom_call", output_to_operand_aliasing={{0}: (7, {}), {1}: (8, {})} | custom-call | flops 38654705664 | bytes 75497472 | tf_op jit(solution)/shard_map/pallas_call | solution.py:239
  554.0 60.4 %shard_map.200 = (f32[1024,1024]{1,0:T(8,128)}, f32[1024,512]{1,0:T(8,128)S(1)}, f32[1024,512]{1,0:T(8,128)}) custom-call(s32[1024,1]{1,0:T(8,128)S(1)} %copy.89.qseq_ref, s32[1,1024]{1,0:T(1,128)S(1)} %bitcast.101, bf16[1024,1024]{1,0:T(8,128)(2,1)} %copy.90.q_ref, bf16[1024,512]{1,0:T(8,128)(2,1)S(1)} %copy-done.1, bf16[1024,512]{1,0:T(8,128)(2,1)S(1)} %copy-done.3, ...), custom_call_target="tpu_custom_call" | custom-call | flops 42949672960 | bytes 20971520 | tf_op jit(solution)/shard_map/pallas_call | solution.py:166
  667.8 33.9 %collective-permute-done.32 = bf16[768,1024]{1,0:T(8,128)(2,1)S(1)} collective-permute-done((bf16[768,1024]{1,0:T(8,128)(2,1)S(1)}, bf16[768,1024]{1,0:T(8,128)(2,1)S(1)}, u32[]{:S(2)}, u32[]{:S(2)}) %collective-permute-start.32) | collective-permute-done | bytes 1572896 | tf_op jit(solution)/shard_map/ppermute | solution.py:271
  702.4 32.8 %collective-permute-done.33 = bf16[1536,1024]{1,0:T(8,128)(2,1)S(1)} collective-permute-done((bf16[1536,1024]{1,0:T(8,128)(2,1)S(1)}, bf16[1536,1024]{1,0:T(8,128)(2,1)S(1)}, u32[]{:S(2)}, u32[]{:S(2)}) %collective-permute-start.33) | collective-permute-done | bytes 3145760 | tf_op jit(solution)/shard_map/ppermute | solution.py:271
  762.8 11.7 collective-permute-done.35
  777.7 30.4 %collective-permute-done.36 = bf16[1536,1024]{1,0:T(8,128)(2,1)} collective-permute-done((bf16[1536,1024]{1,0:T(8,128)(2,1)}, bf16[1536,1024]{1,0:T(8,128)(2,1)}, u32[]{:S(2)}, u32[]{:S(2)}) %collective-permute-start.36) | collective-permute-done | bytes 3145760 | tf_op jit(solution)/shard_map/ppermute | solution.py:271
  842.0 72.1 %collective-permute-done.13 = bf16[528,1024]{1,0:T(8,128)(2,1)} collective-permute-done((bf16[528,1024]{1,0:T(8,128)(2,1)}, bf16[528,1024]{1,0:T(8,128)(2,1)}, u32[]{:S(2)}, u32[]{:S(2)}) %collective-permute-start.13) | collective-permute-done | bytes 1081376 | tf_op jit(solution)/shard_map/ppermute | solution.py:271
  919.1 14.2 %collective-permute-done.37 = bf16[192,1024]{1,0:T(8,128)(2,1)S(1)} collective-permute-done((bf16[192,1024]{1,0:T(8,128)(2,1)S(1)}, bf16[192,1024]{1,0:T(8,128)(2,1)S(1)}, u32[]{:S(2)}, u32[]{:S(2)}) %collective-permute-start.37) | collective-permute-done | bytes 393248 | tf_op jit(solution)/shard_map/ppermute | solution.py:271
  946.1 12.4 %collective-permute-done.25 = bf16[48,1024]{1,0:T(8,128)(2,1)S(1)} collective-permute-done((bf16[48,1024]{1,0:T(8,128)(2,1)S(1)}, bf16[48,1024]{1,0:T(8,128)(2,1)S(1)}, u32[]{:S(2)}, u32[]{:S(2)}) %collective-permute-start.25) | collective-permute-done | bytes 98336 | tf_op jit(solution)/shard_map/ppermute | solution.py:271
  966.1 21.8 %collective-permute-done.42 = bf16[192,1024]{1,0:T(8,128)(2,1)S(1)} collective-permute-done((bf16[192,1024]{1,0:T(8,128)(2,1)S(1)}, bf16[192,1024]{1,0:T(8,128)(2,1)S(1)}, u32[]{:S(2)}, u32[]{:S(2)}) %collective-permute-start.42) | collective-permute-done | bytes 393248 | tf_op jit(solution)/shard_map/ppermute | solution.py:271
  998.1 10.6 collective-permute-done.46
  1008.9 32.3 %collective-permute-done.47 = bf16[192,1024]{1,0:T(8,128)(2,1)S(1)} collective-permute-done((bf16[192,1024]{1,0:T(8,128)(2,1)S(1)}, bf16[192,1024]{1,0:T(8,128)(2,1)S(1)}, u32[]{:S(2)}, u32[]{:S(2)}) %collective-permute-start.47) | collective-permute-done | bytes 393248 | tf_op jit(solution)/shard_map/ppermute | solution.py:271
  1054.8 12.2 collective-permute-done.51
  1067.1 21.4 %collective-permute-done.52 = bf16[192,1024]{1,0:T(8,128)(2,1)S(1)} collective-permute-done((bf16[192,1024]{1,0:T(8,128)(2,1)S(1)}, bf16[192,1024]{1,0:T(8,128)(2,1)S(1)}, u32[]{:S(2)}, u32[]{:S(2)}) %collective-permute-start.52) | collective-permute-done | bytes 393248 | tf_op jit(solution)/shard_map/ppermute | solution.py:271
  1099.7 10.7 collective-permute-done.16
  1153.5 15.6 %collective-permute-done.56 = bf16[768,1024]{1,0:T(8,128)(2,1)S(1)} collective-permute-done((bf16[768,1024]{1,0:T(8,128)(2,1)S(1)}, bf16[768,1024]{1,0:T(8,128)(2,1)S(1)}, u32[]{:S(2)}, u32[]{:S(2)}) %collective-permute-start.56) | collective-permute-done | bytes 1572896 | tf_op jit(solution)/shard_map/ppermute | solution.py:271
  1184.4 26.5 %collective-permute-done.58 = bf16[768,1024]{1,0:T(8,128)(2,1)} collective-permute-done((bf16[768,1024]{1,0:T(8,128)(2,1)}, bf16[768,1024]{1,0:T(8,128)(2,1)}, u32[]{:S(2)}, u32[]{:S(2)}) %collective-permute-start.58) | collective-permute-done | bytes 1572896 | tf_op jit(solution)/shard_map/ppermute | solution.py:271
  (529 shorter events, 409.7 us)
Async XLA Ops:
  57.0 183.6 %collective-permute-start.3 = (bf16[4,1024,1024]{2,1,0:T(8,128)(2,1)}, bf16[4,1024,1024]{2,1,0:T(8,128)(2,1)}, u32[]{:S(2)}, u32[]{:S(2)}) collective-permute-start(bf16[4,1024,1024]{2,1,0:T(8,128)(2,1)} %win_ref), channel_id=1, source_target_pairs={{0,2},{1,3},{2,0},{3,1},{4,6},{5,7},{6,4},{7,5},{8,10},{9,11},{10,... | collective-permute-start | bytes 25165832 | tf_op jit(solution)/shard_map/ppermute | solution.py:271
  72.9 257.1 %collective-permute-start.7 = (bf16[4,1024,1024]{2,1,0:T(8,128)(2,1)}, bf16[4,1024,1024]{2,1,0:T(8,128)(2,1)}, u32[]{:S(2)}, u32[]{:S(2)}) collective-permute-start(bf16[4,1024,1024]{2,1,0:T(8,128)(2,1)} %win_ref), channel_id=1, source_target_pairs={{0,1},{1,0},{2,3},{3,2},{4,5},{5,4},{6,7},{7,6},{8,9},{9,8},{10,11... | collective-permute-start | bytes 25165832 | tf_op jit(solution)/shard_map/ppermute | solution.py:271
  73.1 256.9 %collective-permute-start.8 = (bf16[4,512,1024]{2,1,0:T(8,128)(2,1)}, bf16[4,512,1024]{2,1,0:T(8,128)(2,1)}, u32[]{:S(2)}, u32[]{:S(2)}) collective-permute-start(bf16[4,512,1024]{2,1,0:T(8,128)(2,1)} %wout_ref), channel_id=1, source_target_pairs={{0,1},{1,0},{2,3},{3,2},{4,5},{5,4},{6,7},{7,6},{8,9},{9,8},{10,11... | collective-permute-start | bytes 12582920 | tf_op jit(solution)/shard_map/ppermute | solution.py:271
  73.4 256.6 %collective-permute-start.5 = (bf16[4,512,1024]{2,1,0:T(8,128)(2,1)}, bf16[4,512,1024]{2,1,0:T(8,128)(2,1)}, u32[]{:S(2)}, u32[]{:S(2)}) collective-permute-start(bf16[4,512,1024]{2,1,0:T(8,128)(2,1)} %wout_ref), channel_id=1, source_target_pairs={{0,2},{1,3},{2,0},{3,1},{4,6},{5,7},{6,4},{7,5},{8,10},{9,11},{10,... | collective-permute-start | bytes 12582920 | tf_op jit(solution)/shard_map/ppermute | solution.py:271
  240.5 191.8 %collective-permute-start.4 = (bf16[4,1024,1024]{2,1,0:T(8,128)(2,1)}, bf16[4,1024,1024]{2,1,0:T(8,128)(2,1)}, u32[]{:S(2)}, u32[]{:S(2)}) collective-permute-start(bf16[4,1024,1024]{2,1,0:T(8,128)(2,1)} %collective-permute-done.3.win_ref), channel_id=1, source_target_pairs={{0,1},{1,0},{2,3},{3,2},{4,5},{5,4},{6,7},{7,6},{8,9},{9,8},{10,11... | collective-permute-start | bytes 25165832 | tf_op jit(solution)/shard_map/ppermute | solution.py:271
  330.0 102.3 %collective-permute-start.6 = (bf16[4,512,1024]{2,1,0:T(8,128)(2,1)}, bf16[4,512,1024]{2,1,0:T(8,128)(2,1)}, u32[]{:S(2)}, u32[]{:S(2)}) collective-permute-start(bf16[4,512,1024]{2,1,0:T(8,128)(2,1)} %collective-permute-done.5.wout_ref), channel_id=1, source_target_pairs={{0,1},{1,0},{2,3},{3,2},{4,5},{5,4},{6,7},{7,6},{8,9},{9,8},{10,11... | collective-permute-start | bytes 12582920 | tf_op jit(solution)/shard_map/ppermute | solution.py:271
  380.7 141.7 %collective-permute-start.29 = (bf16[4,1024,1024]{2,1,0:T(8,128)(2,1)}, bf16[4,1024,1024]{2,1,0:T(8,128)(2,1)}, u32[]{:S(2)}, u32[]{:S(2)}) collective-permute-start(bf16[4,1024,1024]{2,1,0:T(8,128)(2,1)} %get-tuple-element.105), channel_id=1, source_target_pairs={{0,1},{1,0},{2,3},{3,2},{4,5},{5,4},{6,7},{7,6},{8,9},{9,8},{10,11... | collective-permute-start | bytes 25165832 | tf_op jit(solution)/shard_map/ppermute | solution.py:271
  381.2 105.4 %collective-permute-start.30 = (bf16[4,512,1024]{2,1,0:T(8,128)(2,1)}, bf16[4,512,1024]{2,1,0:T(8,128)(2,1)}, u32[]{:S(2)}, u32[]{:S(2)}) collective-permute-start(bf16[4,512,1024]{2,1,0:T(8,128)(2,1)} %get-tuple-element.107), channel_id=1, source_target_pairs={{0,1},{1,0},{2,3},{3,2},{4,5},{5,4},{6,7},{7,6},{8,9},{9,8},{10,11... | collective-permute-start | bytes 12582920 | tf_op jit(solution)/shard_map/ppermute | solution.py:271
  483.1 61.5 %collective-permute-start.9 = (bf16[4,1024,1024]{2,1,0:T(8,128)(2,1)}, bf16[4,1024,1024]{2,1,0:T(8,128)(2,1)}, u32[]{:S(2)}, u32[]{:S(2)}) collective-permute-start(bf16[4,1024,1024]{2,1,0:T(8,128)(2,1)} %get-tuple-element.98), channel_id=1, source_target_pairs={{0,1},{1,0},{2,3},{3,2},{4,5},{5,4},{6,7},{7,6},{8,9},{9,8},{10,11... | collective-permute-start | bytes 25165832 | tf_op jit(solution)/shard_map/ppermute | solution.py:271
  552.2 108.2 %collective-permute-start.31 = (bf16[1536,1024]{1,0:T(8,128)(2,1)}, bf16[1536,1024]{1,0:T(8,128)(2,1)}, u32[]{:S(2)}, u32[]{:S(2)}) collective-permute-start(bf16[1536,1024]{1,0:T(8,128)(2,1)} %pad_maximum_fusion.held_ref), channel_id=1, source_target_pairs={{0,2},{1,3},{2,0},{3,1},{4,6},{5,7},{6,4},{7,5},{8,10},{9,11},{10,... | collective-permute-start | bytes 9437192 | tf_op jit(solution)/shard_map/ppermute | solution.py:271
  642.3 108.2 %collective-permute-start.21 = (bf16[384,1024]{1,0:T(8,128)(2,1)}, bf16[384,1024]{1,0:T(8,128)(2,1)}, u32[]{:S(2)}, u32[]{:S(2)}) collective-permute-start(bf16[384,1024]{1,0:T(8,128)(2,1)} %pad_maximum_fusion.25), channel_id=1, source_target_pairs={{0,1},{1,0},{2,3},{3,2},{4,5},{5,4},{6,7},{7,6},{8,9},{9,8},{10,11... | collective-permute-start | bytes 2359304 | tf_op jit(solution)/shard_map/ppermute | solution.py:271
  651.7 160.2 %collective-permute-start.12 = (bf16[528,1024]{1,0:T(8,128)(2,1)}, bf16[528,1024]{1,0:T(8,128)(2,1)}, u32[]{:S(2)}, u32[]{:S(2)}) collective-permute-start(bf16[528,1024]{1,0:T(8,128)(2,1)} %pad_maximum_fusion.21), channel_id=1, source_target_pairs={{0,1},{1,0},{2,3},{3,2},{4,5},{5,4},{6,7},{7,6},{8,9},{9,8},{10,11... | collective-permute-start | bytes 3244040 | tf_op jit(solution)/shard_map/ppermute | solution.py:271
  664.6 70.5 %collective-permute-start.33 = (bf16[1536,1024]{1,0:T(8,128)(2,1)S(1)}, bf16[1536,1024]{1,0:T(8,128)(2,1)S(1)}, u32[]{:S(2)}, u32[]{:S(2)}) collective-permute-start(bf16[1536,1024]{1,0:T(8,128)(2,1)S(1)} %get-tuple-element.110), channel_id=1, source_target_pairs={{0,2},{1,3},{2,0},{3,1},{4,6},{5,7},{6,4},{7,5},{8,10},{9,11},{10,... | collective-permute-start | bytes 9437192 | tf_op jit(solution)/shard_map/ppermute | solution.py:271
  736.7 71.4 %collective-permute-start.36 = (bf16[1536,1024]{1,0:T(8,128)(2,1)}, bf16[1536,1024]{1,0:T(8,128)(2,1)}, u32[]{:S(2)}, u32[]{:S(2)}) collective-permute-start(bf16[1536,1024]{1,0:T(8,128)(2,1)} %get-tuple-element.118), channel_id=1, source_target_pairs={{0,2},{1,3},{2,0},{3,1},{4,6},{5,7},{6,4},{7,5},{8,10},{9,11},{10,... | collective-permute-start | bytes 9437192 | tf_op jit(solution)/shard_map/ppermute | solution.py:271
  750.5 66.0 %collective-permute-start.20 = (bf16[384,1024]{1,0:T(8,128)(2,1)}, bf16[384,1024]{1,0:T(8,128)(2,1)S(1)}, u32[]{:S(2)}, u32[]{:S(2)}) collective-permute-start(bf16[384,1024]{1,0:T(8,128)(2,1)} %pad_maximum_fusion.24), channel_id=1, source_target_pairs={{0,1},{1,0},{2,3},{3,2},{4,5},{5,4},{6,7},{7,6},{8,9},{9,8},{10,11... | collective-permute-start | bytes 2359304 | tf_op jit(solution)/shard_map/ppermute | solution.py:271
  760.0 64.9 %collective-permute-start.22 = (bf16[384,1024]{1,0:T(8,128)(2,1)S(1)}, bf16[384,1024]{1,0:T(8,128)(2,1)S(1)}, u32[]{:S(2)}, u32[]{:S(2)}) collective-permute-start(bf16[384,1024]{1,0:T(8,128)(2,1)S(1)} %maximum_add_fusion.4), channel_id=1, source_target_pairs={{0,2},{1,3},{2,0},{3,1},{4,6},{5,7},{6,4},{7,5},{8,10},{9,11},{10,... | collective-permute-start | bytes 2359304 | tf_op jit(solution)/shard_map/ppermute | solution.py:271
  774.5 67.0 %collective-permute-start.11 = (bf16[528,1024]{1,0:T(8,128)(2,1)}, bf16[528,1024]{1,0:T(8,128)(2,1)}, u32[]{:S(2)}, u32[]{:S(2)}) collective-permute-start(bf16[528,1024]{1,0:T(8,128)(2,1)} %pad_maximum_fusion.20), channel_id=1, source_target_pairs={{0,1},{1,0},{2,3},{3,2},{4,5},{5,4},{6,7},{7,6},{8,9},{9,8},{10,11... | collective-permute-start | bytes 3244040 | tf_op jit(solution)/shard_map/ppermute | solution.py:271
  811.6 126.0 %collective-permute-start.40 = (bf16[1536,1024]{1,0:T(8,128)(2,1)}, bf16[1536,1024]{1,0:T(8,128)(2,1)}, u32[]{:S(2)}, u32[]{:S(2)}) collective-permute-start(bf16[1536,1024]{1,0:T(8,128)(2,1)} %get-tuple-element.125), channel_id=1, source_target_pairs={{0,2},{1,3},{2,0},{3,1},{4,6},{5,7},{6,4},{7,5},{8,10},{9,11},{10,... | collective-permute-start | bytes 9437192 | tf_op jit(solution)/shard_map/ppermute | solution.py:271
  815.6 98.6 %collective-permute-start.13 = (bf16[528,1024]{1,0:T(8,128)(2,1)}, bf16[528,1024]{1,0:T(8,128)(2,1)}, u32[]{:S(2)}, u32[]{:S(2)}) collective-permute-start(bf16[528,1024]{1,0:T(8,128)(2,1)} %maximum_add_fusion.2), channel_id=1, source_target_pairs={{0,2},{1,3},{2,0},{3,1},{4,6},{5,7},{6,4},{7,5},{8,10},{9,11},{10,... | collective-permute-start | bytes 3244040 | tf_op jit(solution)/shard_map/ppermute | solution.py:271
  828.9 106.4 %collective-permute-start.39 = (bf16[768,1024]{1,0:T(8,128)(2,1)}, bf16[768,1024]{1,0:T(8,128)(2,1)}, u32[]{:S(2)}, u32[]{:S(2)}) collective-permute-start(bf16[768,1024]{1,0:T(8,128)(2,1)} %constant_dynamic-slice_fusion.6), channel_id=1, source_target_pairs={{0,4},{4,0},{8,12},{12,8},{16,20},{20,16},{24,28},{28,24},{1,5},{5... | collective-permute-start | bytes 4718600 | tf_op jit(solution)/shard_map/ppermute | solution.py:271
  839.8 95.1 %collective-permute-start.38 = (bf16[384,1024]{1,0:T(8,128)(2,1)S(1)}, bf16[384,1024]{1,0:T(8,128)(2,1)S(1)}, u32[]{:S(2)}, u32[]{:S(2)}) collective-permute-start(bf16[384,1024]{1,0:T(8,128)(2,1)S(1)} %constant_dynamic-slice_fusion.7), channel_id=1, source_target_pairs={{0,8},{4,12},{8,0},{12,4},{16,24},{20,28},{24,16},{28,20},{1,9},{5... | collective-permute-start | bytes 2359304 | tf_op jit(solution)/shard_map/ppermute | solution.py:271
  841.5 100.3 %collective-permute-start.24 = (bf16[96,1024]{1,0:T(8,128)(2,1)S(1)}, bf16[96,1024]{1,0:T(8,128)(2,1)S(1)}, u32[]{:S(2)}, u32[]{:S(2)}) collective-permute-start(bf16[96,1024]{1,0:T(8,128)(2,1)S(1)} %constant_dynamic-slice_fusion.13), channel_id=1, source_target_pairs={{0,8},{4,12},{8,0},{12,4},{16,24},{20,28},{24,16},{28,20},{1,9},{5... | collective-permute-start | bytes 589832 | tf_op jit(solution)/shard_map/ppermute | solution.py:271
  933.3 118.6 %collective-permute-start.14 = (bf16[264,1024]{1,0:T(8,128)(2,1)S(1)}, bf16[264,1024]{1,0:T(8,128)(2,1)S(1)}, u32[]{:S(2)}, u32[]{:S(2)}) collective-permute-start(bf16[264,1024]{1,0:T(8,128)(2,1)S(1)} %constant_dynamic-slice_fusion.21), channel_id=1, source_target_pairs={{0,4},{4,0},{8,12},{12,8},{16,20},{20,16},{24,28},{28,24},{1,5},{5... | collective-permute-start | bytes 1622024 | tf_op jit(solution)/shard_map/ppermute | solution.py:271
  989.2 109.9 %collective-permute-start.27 = (bf16[96,1024]{1,0:T(8,128)(2,1)S(1)}, bf16[96,1024]{1,0:T(8,128)(2,1)S(1)}, u32[]{:S(2)}, u32[]{:S(2)}) collective-permute-start(bf16[96,1024]{1,0:T(8,128)(2,1)S(1)} %pad_maximum_fusion.35), channel_id=1, source_target_pairs={{0,8},{4,12},{8,0},{12,4},{16,24},{20,28},{24,16},{28,20},{1,9},{5... | collective-permute-start | bytes 589832 | tf_op jit(solution)/shard_map/ppermute | solution.py:271
  (126 other events, 2149.2 us)
